TPU v7x, 128 devices: a whole 4x4x4 slice. The times are simulated.
128 devices in a mesh: patch: 16 (over x, y_lo, core), head: 8 (over y_hi, z).
Axes of the slice: x: 4, y: 4 (y_hi: 2, y_lo: 2; y = y_hi * 2 + y_lo), z: 4, core: 2. Of those that a mesh axis runs over, the one named last changes fastest.
Arguments:
- video_in: bfloat16 [2, 4096, 3072], P(None, ('patch', 'head')), may hold values from -6 to 6
- text_in: bfloat16 [2, 256, 3072], P(None, ('patch', 'head')), may hold values from -6 to 6
- video_mod: float32 [2, 3, 3072], replicated, may hold values from -4 to 4
- text_mod: float32 [2, 3, 3072], replicated, may hold values from -4 to 4
- video_qkv: bfloat16 [3, 3072, 2048], P(None, None, 'head'), may hold values from -0.109375 to 0.109375
- text_qkv: bfloat16 [3, 3072, 2048], P(None, None, 'head'), may hold values from -0.109375 to 0.109375
- video_out_w: bfloat16 [2048, 3072], P('head'), may hold values from -0.125 to 0.125
- text_out_w: bfloat16 [2048, 3072], P('head'), may hold values from -0.125 to 0.125
- norm_gains: float32 [4, 128], replicated, may hold values from 0.5 to 20
- stale_kv: bfloat16 [2, 4096, 2048], P(None, 'patch', 'head'), may hold values from -120 to 120
Outputs:
- video_out: bfloat16 [2, 4096, 3072], P(None, ('patch', 'head'))
- text_out: bfloat16 [2, 256, 3072], P(None, ('patch', 'head'))
- fresh_kv: bfloat16 [2, 4096, 2048], P(None, 'patch', 'head')
All inputs are finite; a program needn't handle non-finite values.
Results may differ from a plain program's by a relative error of at most 0.015.
The roundings to bfloat16 on the way count: a program that leaves them out, or rounds other values in their place, can miss the bound.
Values may be sent and summed in bfloat16 or wider, within the bound.
A program may use at most 128 MiB of HBM per device.

v0:
```python
import jax
import jax.numpy as jnp
from jax import lax
from jax.sharding import PartitionSpec as P

HD = 128


EPSILON = 1e-06
MASKED = -1e30


def layer_norm(row_data):
    row_data = row_data.astype(jnp.float32)
    center = row_data - jnp.mean(row_data, axis=-1, keepdims=True)
    return center * lax.rsqrt(jnp.mean(center * center, axis=-1, keepdims=True) + EPSILON)


def modulate(row_data, shift, scale):
    return (layer_norm(row_data) * (1.0 + scale) + shift).astype(jnp.bfloat16)


def head_norm(values, gain_row):
    return (
        values * lax.rsqrt(jnp.mean(values * values, axis=-1, keepdims=True) + EPSILON) * gain_row
    )


def project(normed, weights, query_gain, key_gain):
    projected = jnp.einsum("rd,jdc->jrc", normed, weights, preferred_element_type=jnp.float32)
    separated = projected.reshape(3, normed.shape[0], -1, HD)
    queries = head_norm(separated[0], query_gain).astype(jnp.bfloat16)
    key_rows = head_norm(separated[1], key_gain).astype(jnp.bfloat16)
    return (queries, key_rows, separated[2].astype(jnp.bfloat16))


def prepare(step_index, video_in, text_in, video_mod, text_mod, video_qkv, text_qkv, norm_gains):
    video_normed = modulate(
        video_in[step_index], video_mod[step_index, 0], video_mod[step_index, 1]
    )
    text_normed = modulate(text_in[step_index], text_mod[step_index, 0], text_mod[step_index, 1])
    video_count = video_normed.shape[0]
    block_width = video_count + text_normed.shape[0]
    local_rows = jnp.concatenate([video_normed, text_normed], axis=0)
    gathered = lax.all_gather(local_rows, "head", axis=0, tiled=True)
    blocks = gathered.reshape(-1, block_width, gathered.shape[1])
    groups = blocks.shape[0]
    video_part = blocks[:, :video_count].reshape(-1, blocks.shape[2])
    text_part = blocks[:, video_count:].reshape(-1, blocks.shape[2])
    video_query, video_key, video_value = project(
        video_part, video_qkv, norm_gains[0], norm_gains[1]
    )
    text_query, text_key, text_value = project(text_part, text_qkv, norm_gains[2], norm_gains[3])
    heads_local = video_query.shape[1]
    queries = jnp.concatenate(
        [
            video_query.reshape(groups, video_count, heads_local, HD),
            text_query.reshape(groups, -1, heads_local, HD),
        ],
        axis=1,
    )
    queries = queries.reshape(-1, heads_local, HD)
    fresh_video = jnp.stack([video_key, video_value]).reshape(2, video_part.shape[0], -1)
    fresh_text = jnp.stack([text_key, text_value]).reshape(2, text_part.shape[0], -1)
    return (queries, fresh_video, fresh_text)


def start_online(queries):
    row_count, heads_local = (queries.shape[0], queries.shape[1])
    return (
        jnp.full((heads_local, row_count), MASKED, jnp.float32),
        jnp.zeros((heads_local, row_count), jnp.float32),
        jnp.zeros((heads_local, row_count, HD), jnp.float32),
    )


def fold_block(online, pieces, queries, own_first, own_last):
    running_max, running_sum, running_acc = online
    length = pieces.shape[1]
    heads_local = queries.shape[1]
    key_rows = pieces[0].reshape(length, heads_local, HD)
    value_rows = pieces[1].reshape(length, heads_local, HD)
    scores = jnp.einsum(
        "rhd,nhd->hrn", queries, key_rows, preferred_element_type=jnp.float32
    ) * HD ** (-0.5)
    position = jnp.arange(length, dtype=jnp.int32)
    visible = (position < own_first) | (position >= own_last)
    scores = jnp.where(visible[None, None, :], scores, MASKED)
    highest = jnp.maximum(running_max, jnp.max(scores, axis=2))
    shrink = jnp.exp(running_max - highest)
    weights = jnp.exp(scores - highest[:, :, None])
    running_sum = running_sum * shrink + jnp.sum(weights, axis=2)
    running_acc = running_acc * shrink[:, :, None] + jnp.einsum(
        "hrn,nhd->hrd", weights.astype(jnp.bfloat16), value_rows, preferred_element_type=jnp.float32
    )
    return (highest, running_sum, running_acc)


def gather_text(fresh_text):
    return lax.all_gather(fresh_text, "patch", axis=1, tiled=True)


def fold_remote(online, stale_pairs, queries, own_first, own_last):
    return fold_block(
        online,
        lax.all_gather(stale_pairs, "patch", axis=1, tiled=True),
        queries,
        own_first,
        own_last,
    )


def finish(online, step_index, video_in, text_in, video_mod, text_mod, video_out_w, text_out_w):
    running_max, running_sum, running_acc = online
    context = (running_acc / running_sum[:, :, None]).astype(jnp.bfloat16)
    video_count = video_in.shape[1]
    block_width = video_count + text_in.shape[1]
    heads_local = context.shape[0]
    video_weight = video_out_w.reshape(heads_local, HD, -1)
    text_weight = text_out_w.reshape(heads_local, HD, -1)
    sliced = context
    sliced = sliced.reshape(
        heads_local, block_width * lax.axis_size("head") // block_width, block_width, HD
    )
    video_term = jnp.einsum(
        "hgrk,hkd->grd",
        sliced[:, :, :video_count],
        video_weight,
        preferred_element_type=jnp.float32,
    )
    text_term = jnp.einsum(
        "hgrk,hkd->grd", sliced[:, :, video_count:], text_weight, preferred_element_type=jnp.float32
    )
    summed = lax.psum_scatter(
        jnp.concatenate([video_term, text_term], axis=1)
        .reshape(block_width * lax.axis_size("head"), -1)
        .astype(jnp.bfloat16),
        "head",
        scatter_dimension=0,
        tiled=True,
    ).astype(jnp.float32)
    video_new = (
        video_in[step_index].astype(jnp.float32) + video_mod[step_index, 2] * summed[:video_count]
    ).astype(jnp.bfloat16)
    text_new = (
        text_in[step_index].astype(jnp.float32) + text_mod[step_index, 2] * summed[video_count:]
    ).astype(jnp.bfloat16)
    return (video_new, text_new)


def shards(
    video_in,
    text_in,
    video_mod,
    text_mod,
    video_qkv,
    text_qkv,
    video_out_w,
    text_out_w,
    norm_gains,
    stale_kv,
):
    video_list = []
    text_list = []
    group_rows = stale_kv.shape[1]
    own_first = lax.axis_index("patch") * group_rows
    own_last = own_first + group_rows
    step_total = video_in.shape[0]
    stale_pairs = stale_kv
    for step_index in range(step_total):
        queries, fresh_video, fresh_text = prepare(
            step_index, video_in, text_in, video_mod, text_mod, video_qkv, text_qkv, norm_gains
        )
        online = fold_block(start_online(queries), fresh_video, queries, 0, 0)
        text_all = gather_text(fresh_text)
        online = fold_block(online, text_all, queries, 0, 0)
        online = fold_remote(online, stale_pairs, queries, own_first, own_last)
        stale_pairs = fresh_video
        video_new, text_new = finish(
            online, step_index, video_in, text_in, video_mod, text_mod, video_out_w, text_out_w
        )
        video_list.append(video_new)
        text_list.append(text_new)
    return (jnp.stack(video_list), jnp.stack(text_list), fresh_video)


def solution(mesh):
    return jax.shard_map(
        shards,
        mesh=mesh,
        in_specs=(
            P(None, ("patch", "head"), None),
            P(None, ("patch", "head"), None),
            P(),
            P(),
            P(None, None, "head"),
            P(None, None, "head"),
            P("head", None),
            P("head", None),
            P(),
            P(None, "patch", "head"),
        ),
        out_specs=(
            P(None, ("patch", "head"), None),
            P(None, ("patch", "head"), None),
            P(None, "patch", "head"),
        ),
        check_vma=False,
    )
```

profile of v0, /device:TPU:0, one launch (start us, length us, event | category | flops | bytes accessed | tf_op | source)
XLA Modules:
  0.0 327.4 jit_solution(9153346529396500191)
XLA Ops:
  7.2 1.3 convert_reduce_fusion
  8.6 1.3 fusion.42
  9.9 0.9 convert_reduce_fusion.2
  10.8 1.0 fusion.92
  11.8 1.5 fusion.123
  13.3 1.5 fusion.122
  14.8 0.8 fusion.95
  15.6 1.2 fusion.45
  18.5 0.8 copy.91
  21.2 52.0 %all-gather.11.cloned.1.call-done = bf16[8,34,3072]{2,1,0:T(8,128)(2,1)} async-done(((bf16[1,34,3072]{2,1,0:T(8,128)(2,1)}), bf16[8,34,3072]{2,1,0:T(8,128)(2,1)}) %all-gather.11.cloned.1.call-update) | async-done | bytes 1671184 | tf_op jit(solution)/shard_map/all_gather | solution.py:45
  73.2 1.4 slice-done.1
  74.6 4.3 %convolution_bitcast_fusion.5 = f32[3,256,256]{1,2,0:T(8,128)S(1)} fusion(bf16[256,3072,1]{1,0,2:T(8,128)(2,1)S(1)} %bitcast.230, bf16[3,3072,256]{2,1,0:T(8,128)(2,1)} %param.14), kind=kOutput, calls=%fused_computation.23 | convolution fusion | flops 1207959552 | bytes 7077888 | tf_op jit(solution)/shard_map/rd,jdc->jrc/dot_general | solution.py:30
  79.0 0.9 copy-done.11
  79.9 46.3 %all-gather.13.cloned.1.call-done = bf16[8,34,3072]{2,1,0:T(8,128)(2,1)} async-done(((bf16[1,34,3072]{2,1,0:T(8,128)(2,1)}), bf16[8,34,3072]{2,1,0:T(8,128)(2,1)}) %all-gather.13.cloned.1.call-update) | async-done | bytes 1671184 | tf_op jit(solution)/shard_map/all_gather | solution.py:45
  126.2 1.8 slice.255
  128.0 1.6 reshape.478
  129.5 4.4 %convolution_bitcast_fusion.4 = f32[3,256,256]{1,2,0:T(8,128)S(1)} fusion(bf16[256,3072,1]{1,0,2:T(8,128)(2,1)S(1)} %bitcast.229, bf16[3,3072,256]{2,1,0:T(8,128)(2,1)} %param.14), kind=kOutput, calls=%fused_computation.22 | convolution fusion | flops 1207959552 | bytes 7077888 | tf_op jit(solution)/shard_map/rd,jdc->jrc/dot_general | solution.py:30
  136.4 3.1 convolution_bitcast_fusion.6
  139.4 1.6 slice.330
  141.9 0.8 copy.104
  143.0 1.1 slice.240
  144.1 3.1 convolution_bitcast_fusion.7
  147.7 19.8 %all_gather.19 = bf16[2,256,256]{2,1,0:T(8,128)(2,1)S(1)} all-gather(bf16[2,16,256]{2,1,0:T(8,128)(2,1)S(1)} %pad_maximum_fusion.8), channel_id=1, replica_groups=mesh['patch'=16,'head'=8] {'patch'}, dimensions={1}, use_global_device_ids=true | all-gather | bytes 278528 | tf_op jit(solution)/shard_map/all_gather | solution.py:100
  168.9 17.1 %all_gather.22 = bf16[2,256,256]{2,1,0:T(8,128)(2,1)S(1)} all-gather(bf16[2,16,256]{2,1,0:T(8,128)(2,1)S(1)} %pad_maximum_fusion.9), channel_id=1, replica_groups=mesh['patch'=16,'head'=8] {'patch'}, dimensions={1}, use_global_device_ids=true | all-gather | bytes 278528 | tf_op jit(solution)/shard_map/all_gather | solution.py:100
  189.6 1.0 fusion.126
  190.6 2.0 fusion.124
  192.6 1.4 fusion.127
  194.0 1.4 fusion.125
  195.5 2.7 fusion.118
  198.2 1.7 fusion.2
  201.2 2.2 copy-done.1
  203.4 2.6 fusion.10
  206.1 13.0 %all-gather.9.cloned.1.call-done = bf16[2,4096,256]{1,2,0:T(8,128)(2,1)} async-done(((bf16[2,256,256]{1,2,0:T(8,128)(2,1)}), bf16[2,4096,256]{1,2,0:T(8,128)(2,1)}) %all-gather.9.cloned.1.call-update) | async-done | bytes 4194320 | tf_op jit(solution)/shard_map/all_gather | solution.py:106
  219.0 2.7 fusion.119
  221.8 6.5 %fusion.4 = (f32[2,272]{1,0:T(2,128)S(1)}, f32[2,272]{1,0:T(2,128)S(1)}, f32[2,272,4096]{2,1,0:T(8,128)S(1)}) fusion(f32[2,272,4096]{2,1,0:T(8,128)} %copy-done.1, f32[2,272]{1,0:T(2,128)S(1)} %copy-done.29, pred[4096]{0:T(1024)(128)(4,1)S(1)} %fusion.102, bf16[4096,2,128]{0,2,1:T(8,128)(2,1)S(1)} %bitcast.228, bf16[272,2,128]{2,1,0:T(2,128)(2,1)S(1)} %bitcast.233), kind=kOutput, calls=%fused_computation.6 | convolution fusion | flops 586021888 | bytes 20072832 | tf_op jit(solution)/shard_map/rhd,nhd->hrn/dot_general | solution.py:83
  229.9 2.0 fusion.6
  232.0 1.9 fusion.8
  237.7 1.5 convert_element_type.200
  239.1 1.5 fusion.14
  240.9 1.4 convert_element_type.180
  242.3 51.6 %fusion.113 = (bf16[40,3072]{1,0:T(8,128)(2,1)S(1)}, bf16[40,3072]{1,0:T(8,128)(2,1)S(1)}) fusion(bf16[272,3072]{1,0:T(8,128)(2,1)} %convert_element_type.200, bf16[272,3072]{1,0:T(8,128)(2,1)} %convert_element_type.180), kind=kCustom, calls=%all-reduce-scatter.2 | all-reduce-scatter fusion | flops 1966081 | bytes 3834368
  294.0 4.0 %collective-permute-start.2 = (bf16[40,3072]{1,0:T(8,128)(2,1)S(1)}, bf16[40,3072]{1,0:T(8,128)(2,1)}, u32[]{:S(2)}, u32[]{:S(2)}) collective-permute-start(bf16[40,3072]{1,0:T(8,128)(2,1)S(1)} %get-tuple-element.24), channel_id=1, source_target_pairs={{0,1},{1,2},{2,3},{3,4},{4,5},{5,6},{6,7},{8,9},{9,10},{10,11},{11... | collective-permute-start | bytes 737288
  299.3 1.3 collective-permute-start.3
  300.6 0.8 copy.119
  302.1 7.1 %collective-permute-start = (bf16[40,3072]{1,0:T(8,128)(2,1)S(1)}, bf16[40,3072]{1,0:T(8,128)(2,1)}, u32[]{:S(2)}, u32[]{:S(2)}) collective-permute-start(bf16[40,3072]{1,0:T(8,128)(2,1)S(1)} %get-tuple-element.25), channel_id=1, source_target_pairs={{0,1},{1,2},{2,3},{3,4},{4,5},{5,6},{6,7},{8,9},{9,10},{10,11},{11... | collective-permute-start | bytes 737288
  309.1 2.4 collective-permute-start.1
  312.2 3.1 concatenate.31
  315.4 3.1 concatenate.30
  (192 shorter events, 23.4 us)
Async XLA Ops:
  7.2 229.7 %copy-start = (bf16[256,3072]{1,0:T(8,128)(2,1)S(1)}, bf16[256,3072]{1,0:T(8,128)(2,1)}, u32[]{:S(2)}) copy-start(bf16[256,3072]{1,0:T(8,128)(2,1)} %param.16) | copy-start | bytes 4718596
  7.2 11.3 %copy-start.18 = (bf16[2,256,256]{2,1,0:T(8,128)(2,1)S(1)}, bf16[2,256,256]{2,1,0:T(8,128)(2,1)}, u32[]{:S(2)}) copy-start(bf16[2,256,256]{2,1,0:T(8,128)(2,1)} %param.19) | copy-start | bytes 786436
  7.2 12.2 %copy-start.35 = (f32[4,128]{1,0:T(4,128)S(1)}, f32[4,128]{1,0:T(4,128)}, u32[]{:S(2)}) copy-start(f32[4,128]{1,0:T(4,128)} %param.18) | copy-start | bytes 6148
  7.2 66.0 %all-gather.11.cloned.1.call-start = ((), (), s32[]{:S(2)}) async-start(), calls=%async_computation.2 | async-start | bytes 2211840 | tf_op jit(solution)/shard_map/all_gather | solution.py:45
  17.6 108.5 %all-gather.13.cloned.1.call-start = ((), (), s32[]{:S(2)}) async-start(), calls=%async_computation.3 | async-start | bytes 2211840 | tf_op jit(solution)/shard_map/all_gather | solution.py:45
  18.4 177.1 %all-gather.7.cloned.1.call-start = ((), (), s32[]{:S(2)}) async-start(), calls=%async_computation | async-start | bytes 4456448 | tf_op jit(solution)/shard_map/all_gather | solution.py:106
  19.4 199.7 %all-gather.9.cloned.1.call-start = ((), (), s32[]{:S(2)}) async-start(), calls=%async_computation.1 | async-start | bytes 4456448 | tf_op jit(solution)/shard_map/all_gather | solution.py:106
  20.0 0.6 copy-start.30
  73.2 1.4 slice-start.1
  78.9 1.0 copy-start.11
  78.9 56.6 %copy-start.8 = (bf16[1,256,256]{1,2,0:T(8,128)(2,1)}, bf16[1,256,256]{1,2,0:T(8,128)(2,1)S(1)}, u32[]{:S(2)}) copy-start(bf16[1,256,256]{1,2,0:T(8,128)(2,1)S(1)} %slice.331) | copy-start | bytes 393220
  126.2 3.4 %slice-start = ((bf16[8,34,3072]{2,1,0:T(8,128)(2,1)}), bf16[8,32,3072]{2,1,0:T(8,128)(2,1)S(1)}, s32[]{:S(2)}) async-start(bf16[8,34,3072]{2,1,0:T(8,128)(2,1)} %all-gather.13.cloned.1.call-done), calls=%async_computation.4 | async-start | bytes 3145728 | tf_op jit(solution)/shard_map/slice | solution.py:48
  129.5 5.3 %copy-start.12 = (f32[3,256,256]{1,2,0:T(8,128)S(1)}, f32[3,256,256]{1,2,0:T(8,128)}, u32[]{:S(2)}) copy-start(f32[3,256,256]{1,2,0:T(8,128)} %copy-done.11) | copy-start | bytes 2359300
  129.5 5.3 %copy-start.32 = (f32[256]{0:T(256)S(1)}, f32[256]{0:T(256)}, u32[]{:S(2)}) copy-start(f32[256]{0:T(256)} %get-tuple-element.109) | copy-start | bytes 3076
  133.9 0.9 copy-start.10
  133.9 2.4 copy-start.16
  134.0 5.4 %copy-start.23 = (f32[256,2]{0,1:T(2,128)}, f32[256,2]{0,1:T(2,128)S(1)}, u32[]{:S(2)}) copy-start(f32[256,2]{0,1:T(2,128)S(1)} %add_rsqrt_fusion.6) | copy-start | bytes 6148
  134.1 5.4 %copy-start.24 = (f32[256,2]{0,1:T(2,128)}, f32[256,2]{0,1:T(2,128)S(1)}, u32[]{:S(2)}) copy-start(f32[256,2]{0,1:T(2,128)S(1)} %add_rsqrt_fusion.4) | copy-start | bytes 6148
  141.9 5.5 %copy-start.31 = (f32[256]{0:T(256)S(1)}, f32[256]{0:T(256)}, u32[]{:S(2)}) copy-start(f32[256]{0:T(256)} %get-tuple-element.110) | copy-start | bytes 3076
  147.1 41.3 %copy-start.34 = (f32[128]{0:T(128)S(1)}, f32[128]{0:T(128)}, u32[]{:S(2)}) copy-start(f32[128]{0:T(128)} %get-tuple-element.81) | copy-start | bytes 1540
  147.1 41.4 %copy-start.33 = (f32[128]{0:T(128)S(1)}, f32[128]{0:T(128)}, u32[]{:S(2)}) copy-start(f32[128]{0:T(128)} %get-tuple-element.82) | copy-start | bytes 1540
  187.9 1.7 copy-start.13
  198.2 2.7 copy-start.4
  200.0 3.4 %copy-start.1 = (f32[2,272,4096]{2,1,0:T(8,128)}, f32[2,272,4096]{2,1,0:T(8,128)S(1)}, u32[]{:S(2)}) copy-start(f32[2,272,4096]{2,1,0:T(8,128)S(1)} %get-tuple-element.95) | copy-start | bytes 26738692
  200.6 5.4 %copy-start.28 = (f32[2,272]{1,0:T(2,128)}, f32[2,272]{1,0:T(2,128)S(1)}, u32[]{:S(2)}) copy-start(f32[2,272]{1,0:T(2,128)S(1)} %get-tuple-element.34) | copy-start | bytes 6532
  219.0 2.7 copy-start.29
  221.7 6.6 %copy-start.9 = (bf16[1,256,256]{1,2,0:T(8,128)(2,1)S(1)}, bf16[1,256,256]{1,2,0:T(8,128)(2,1)}, u32[]{:S(2)}) copy-start(bf16[1,256,256]{1,2,0:T(8,128)(2,1)} %copy-done.8) | copy-start | bytes 393220
  221.8 6.6 %copy-start.27 = (f32[2,272]{1,0:T(2,128)S(1)}, f32[2,272]{1,0:T(2,128)}, u32[]{:S(2)}) copy-start(f32[2,272]{1,0:T(2,128)} %get-tuple-element.76) | copy-start | bytes 6532
  221.8 6.9 %copy-start.5 = (f32[2,272,256]{2,1,0:T(8,128)S(1)}, f32[2,272,256]{2,1,0:T(8,128)}, u32[]{:S(2)}) copy-start(f32[2,272,256]{2,1,0:T(8,128)} %get-tuple-element.97) | copy-start | bytes 1671172
  221.8 6.9 %copy-start.20 = (bf16[256,2,128]{2,1,0:T(2,128)(2,1)S(1)}, bf16[256,2,128]{2,1,0:T(2,128)(2,1)}, u32[]{:S(2)}) copy-start(bf16[256,2,128]{2,1,0:T(2,128)(2,1)} %reshape_squeeze.29) | copy-start | bytes 393220
  221.8 6.9 %copy-start.37 = (f32[2,272,128]{2,1,0:T(8,128)S(1)}, f32[2,272,128]{2,1,0:T(8,128)}, u32[]{:S(2)}) copy-start(f32[2,272,128]{2,1,0:T(8,128)} %fusion.10) | copy-start | bytes 835588
  228.3 1.6 copy-start.26
  231.9 2.6 copy-start.6
  231.9 2.9 copy-start.19
  233.9 1.5 copy-start.2
  239.1 1.5 copy-start.17
  240.9 57.2 %copy-start.36 = (u32[128]{0:T(128)S(1)}, u32[128]{0:T(128)}, u32[]{:S(2)}) copy-start(u32[128]{0:T(128)} %constant.56) | copy-start | bytes 1540
  242.3 58.3 %copy-start.7 = (bf16[1,256,256]{1,2,0:T(8,128)(2,1)S(1)}, bf16[1,256,256]{1,2,0:T(8,128)(2,1)}, u32[]{:S(2)}) copy-start(bf16[1,256,256]{1,2,0:T(8,128)(2,1)} %slice.330) | copy-start | bytes 393220
  242.3 58.3 %copy-start.14 = (bf16[1,256,256]{1,2,0:T(8,128)(2,1)S(1)}, bf16[1,256,256]{1,2,0:T(8,128)(2,1)}, u32[]{:S(2)}) copy-start(bf16[1,256,256]{1,2,0:T(8,128)(2,1)} %get-tuple-element.86) | copy-start | bytes 393220
  294.0 24.6 %copy-start.15 = (bf16[2,2,3072]{2,1,0:T(2,128)(2,1)S(1)}, bf16[2,2,3072]{2,1,0:T(2,128)(2,1)}, u32[]{:S(2)}) copy-start(bf16[2,2,3072]{2,1,0:T(2,128)(2,1)} %param.11) | copy-start | bytes 73732
  294.0 24.6 %copy-start.22 = (f32[1,1,3072]{2,0,1:T(1,128)S(1)}, f32[1,1,3072]{2,0,1:T(1,128)}, u32[]{:S(2)}) copy-start(f32[1,1,3072]{2,0,1:T(1,128)} %get-tuple-element.54) | copy-start | bytes 36868
  294.0 25.3 %copy-start.3 = (bf16[2,32,3072]{2,1,0:T(8,128)(2,1)S(1)}, bf16[2,32,3072]{2,1,0:T(8,128)(2,1)}, u32[]{:S(2)}) copy-start(bf16[2,32,3072]{2,1,0:T(8,128)(2,1)} %param.10) | copy-start | bytes 1179652
  294.0 25.3 %copy-start.21 = (f32[1,1,3072]{2,0,1:T(1,128)S(1)}, f32[1,1,3072]{2,0,1:T(1,128)}, u32[]{:S(2)}) copy-start(f32[1,1,3072]{2,0,1:T(1,128)} %get-tuple-element.61) | copy-start | bytes 36868
  294.0 18.2 %collective-permute-start.2 = (bf16[40,3072]{1,0:T(8,128)(2,1)S(1)}, bf16[40,3072]{1,0:T(8,128)(2,1)}, u32[]{:S(2)}, u32[]{:S(2)}) collective-permute-start(bf16[40,3072]{1,0:T(8,128)(2,1)S(1)} %get-tuple-element.24), channel_id=1, source_target_pairs={{0,1},{1,2},{2,3},{3,4},{4,5},{5,6},{6,7},{8,9},{9,10},{10,11},{11... | collective-permute-start | bytes 737288
  299.3 12.3 %collective-permute-start.3 = (bf16[2,3072]{1,0:T(2,128)(2,1)S(1)}, bf16[2,3072]{1,0:T(2,128)(2,1)S(1)}, u32[]{:S(2)}, u32[]{:S(2)}) collective-permute-start(bf16[2,3072]{1,0:T(2,128)(2,1)S(1)} %slice.271), channel_id=1, source_target_pairs={{0,2},{1,3},{2,4},{3,5},{4,6},{5,7},{8,10},{9,11},{10,12},{11,13},... | collective-permute-start | bytes 36872
  302.1 13.3 %collective-permute-start = (bf16[40,3072]{1,0:T(8,128)(2,1)S(1)}, bf16[40,3072]{1,0:T(8,128)(2,1)}, u32[]{:S(2)}, u32[]{:S(2)}) collective-permute-start(bf16[40,3072]{1,0:T(8,128)(2,1)S(1)} %get-tuple-element.25), channel_id=1, source_target_pairs={{0,1},{1,2},{2,3},{3,4},{4,5},{5,6},{6,7},{8,9},{9,10},{10,11},{11... | collective-permute-start | bytes 737288
  309.1 6.2 %collective-permute-start.1 = (bf16[2,3072]{1,0:T(2,128)(2,1)}, bf16[2,3072]{1,0:T(2,128)(2,1)}, u32[]{:S(2)}, u32[]{:S(2)}) collective-permute-start(bf16[2,3072]{1,0:T(2,128)(2,1)} %slice.270), channel_id=1, source_target_pairs={{0,2},{1,3},{2,4},{3,5},{4,6},{5,7},{8,10},{9,11},{10,12},{11,13},... | collective-permute-start | bytes 36872
  311.6 0.6 copy-start.25
Sparse Core Ops, SparseCore 0:
  17.7 55.3 all-gather.10
  75.5 50.6 all-gather.12
  128.4 43.3 all-gather.6
  173.8 45.1 all-gather.8
where the time goes:
time: 329 us; the launch traced here: 327 us
  waiting for transfers between devices  111 us (34%)
  blocking collectives  88.5 us (27%)
  local copies, waits for them, and re-layouts  38.7 us (12%)
  matrix products  37.4 us (11%)
  other arithmetic  21 us (6%)
  between operations  15.4 us (5%)
  starting transfers between devices  14.9 us (5%)
    all_gather x2, waiting for transfers between devices, prepare(): gathered = lax.all_gather(local_rows, 'head', axis=0, tiled=True)  98.3 us
    unnamed x1, blocking collectives  51.6 us
    all_gather x2, blocking collectives, gather_text(): return lax.all_gather(fresh_text, 'patch', axis=1, tiled=True)  36.9 us
    dot_general x4, matrix products, project(): jnp.einsum('rd,jdc->jrc', normed, weights, preferred_element_type=jnp.flo...  14.8 us
    unnamed x4, starting transfers between devices  14.8 us
    unnamed x83, local copies, waits for them, and re-layouts  14.2 us
    dot_general x6, matrix products, fold_block(): jnp.einsum('rhd,nhd->hrn', queries, key_rows, preferred_element_type=jnp....  14.1 us
    all_gather x2, waiting for transfers between devices, fold_remote(): lax.all_gather(stale_pairs, 'patch', axis=1, tiled=True)  13 us
  transfers between devices with their start and end apart: 8, of which 3 were waited for; matrix products, arithmetic and copies ran while one was open for 16% of the time, Pallas kernels for 0%

commit v1 on v0

v1 whole, which is shorter than its diff:
```python
import functools

import jax
import jax.numpy as jnp
from jax import lax
from jax.experimental import pallas as pl
from jax.experimental.pallas import tpu as pltpu
from jax.sharding import PartitionSpec as P

HD = 128
EPSILON = 1e-06
MESH = pl.DeviceIdType.MESH
F32 = jnp.float32
BF16 = jnp.bfloat16
EXP2_SCALE = HD ** (-0.5) * 1.4426950408889634

D = 3072
HALF = D // 2
ROWS = 32
VID = 256
TXT = 16
QROWS = VID + TXT
PIECE = 768

FIRST, SECOND = pl.ds(0, HALF), pl.ds(HALF, HALF)


def modulated(rows, shift, scale):
    rows = rows.astype(F32)
    center = rows - jnp.mean(rows, axis=-1, keepdims=True)
    normed = center * lax.rsqrt(jnp.mean(center * center, axis=-1, keepdims=True) + EPSILON)
    return normed * (1.0 + scale) + shift


def head_norm(values, gain_row):
    return (
        values * lax.rsqrt(jnp.mean(values * values, axis=-1, keepdims=True) + EPSILON) * gain_row
    )


def piece_select(piece, transposed):
    shape = (128, 32) if transposed else (32, 128)
    row = lax.broadcasted_iota(jnp.int32, shape, 1 if transposed else 0)
    packed = lax.broadcasted_iota(jnp.int32, shape, 0 if transposed else 1)
    target = ((row & 15) >> 1) * 16 + 4 * piece + 2 * (row >> 4) + (row & 1)
    return jnp.where(packed == target, 1.0, 0.0).astype(BF16)


def slot_of(dz, fy):
    return (dz % 4) * 2 + fy


def group_of(dx, fy, fc):
    return (dx % 4) * 4 + fy * 2 + fc


def kernel(
    video_in,
    text_in,
    video_mod,
    text_mod,
    video_qkv,
    text_qkv,
    video_out_w,
    text_out_w,
    norm_gains,
    stale_kv,
    video_out,
    text_out,
    fresh_kv,
    wv,
    wt,
    wov,
    wot,
    xg,
    tpack,
    tg,
    tx,
    q_ref,
    own_stale,
    kvb,
    tkv,
    m_ref,
    l_ref,
    acc_ref,
    ctx,
    ctxt,
    pbuf,
    half_in,
    full_in,
    last_in,
    tp,
    trx,
    send_sem,
    recv_sem,
    local_sem,
    out_sem,
):
    p = lax.axis_index("patch")
    h = lax.axis_index("head")
    x, yl, c = p // 4, (p // 2) % 2, p % 2
    yh, z = h // 4, h % 4

    def at(dx=0, fy=0, fc=0, fh=0, dz=0):
        xx = (x + dx) % 4 if dx else x
        yy = 1 - yl if fy else yl
        cc = 1 - c if fc else c
        hh = 1 - yh if fh else yh
        zz = (z + dz) % 4 if dz else z
        return (xx * 4 + yy * 2 + cc, hh * 4 + zz)

    table = {}

    def message(name, src, dst, device):
        index = len(table)

        def make():
            return pltpu.make_async_remote_copy(
                src_ref=src,
                dst_ref=dst,
                send_sem=send_sem.at[index],
                recv_sem=recv_sem.at[index],
                device_id=device,
                device_id_type=MESH,
            )

        table[name] = make

    def start(*names):
        for name in names:
            table[name]().start()

    def arrived(*names):
        for name in names:
            table[name]().wait_recv()

    zp, zm, yp = at(dz=1), at(dz=3), at(fh=1)
    xp, xm, ylp, sib = at(dx=1), at(dx=3), at(fy=1), at(fc=1)

    for s in range(2):
        def rows(dz, fy, s=s):
            return xg.at[s, pl.ds(slot_of(dz, fy) * ROWS, ROWS), :]

        def part(dz, fy, cols, s=s):
            return xg.at[s, pl.ds(slot_of(dz, fy) * ROWS, ROWS), cols]

        message(("ag", s, 0), rows(0, 0), rows(0, 1), yp)
        message(("ag", s, 1), rows(0, 0), rows(3, 0), zp)
        message(("ag", s, 2), rows(0, 0), rows(1, 0), zm)
        message(("ag", s, 3), rows(0, 1), rows(3, 1), zp)
        message(("ag", s, 4), rows(0, 1), rows(1, 1), zm)
        message(("ag", s, 5), part(3, 0, FIRST), part(2, 0, FIRST), zp)
        message(("ag", s, 6), part(1, 0, SECOND), part(2, 0, SECOND), zm)
        message(("ag", s, 7), part(3, 1, FIRST), part(2, 1, FIRST), zp)
        message(("ag", s, 8), part(1, 1, SECOND), part(2, 1, SECOND), zm)

    def gather_patch(kind, own, block):
        def half(dx, fy, which):
            return block(dx, fy, 0).at[which]

        message((kind, 0), own, block(0, 0, 1), sib)
        message((kind, 1), own, block(0, 1, 0), ylp)
        message((kind, 2), own, block(3, 0, 0), xp)
        message((kind, 3), own, block(1, 0, 0), xm)
        message((kind, 4), block(0, 1, 0), block(0, 1, 1), sib)
        message((kind, 5), block(0, 1, 0), block(3, 1, 0), xp)
        message((kind, 6), block(0, 1, 0), block(1, 1, 0), xm)
        message((kind, 7), block(3, 0, 0), block(3, 0, 1), sib)
        message((kind, 8), half(3, 0, 0), half(2, 0, 0), xp)
        message((kind, 9), block(1, 0, 0), block(1, 0, 1), sib)
        message((kind, 10), half(1, 0, 1), half(2, 0, 1), xm)
        message((kind, 11), block(3, 1, 0), block(3, 1, 1), sib)
        message((kind, 12), half(3, 1, 0), half(2, 1, 0), xp)
        message((kind, 13), block(1, 1, 0), block(1, 1, 1), sib)
        message((kind, 14), half(1, 1, 1), half(2, 1, 1), xm)
        message((kind, 15), block(2, 0, 0), block(2, 0, 1), sib)
        message((kind, 16), block(2, 1, 0), block(2, 1, 1), sib)

    gather_patch("kv0", own_stale, lambda dx, fy, fc: kvb.at[0, group_of(dx, fy, fc)])
    gather_patch("kv1", kvb.at[1, 0], lambda dx, fy, fc: kvb.at[1, group_of(dx, fy, fc)])
    gather_patch("tkv", tkv.at[0], lambda dx, fy, fc: tkv.at[group_of(dx, fy, fc)])

    def patch_event(kind, number):
        waits, sends = [
            ((1,), (5, 6, 4)),
            ((2, 3), (8, 10, 7, 9)),
            ((5, 6), (12, 14, 11, 13)),
            ((8, 10), (15,)),
            ((12, 14), (16,)),
        ][number]
        arrived(*[(kind, i) for i in waits])
        start(*[(kind, i) for i in sends])

    others = [(dz, fy) for dz in range(4) for fy in range(2) if (dz, fy) != (0, 0)]
    for dz, fy in others:
        message(("ta", dz, fy), tg.at[0], tg.at[slot_of(-dz, fy)], at(fh=fy, dz=dz))
    for dz, fy in others:
        message(
            ("tr", dz, fy), tp.at[slot_of(dz, fy)], trx.at[slot_of(-dz, fy)], at(fh=fy, dz=dz)
        )

    for s in range(2):
        for fy in range(2):
            def summand(dz, s=s, fy=fy):
                return pbuf.at[s, pl.ds(slot_of(dz, fy) * ROWS, ROWS), :]

            def summand_part(dz, cols, s=s, fy=fy):
                return pbuf.at[s, pl.ds(slot_of(dz, fy) * ROWS, ROWS), cols]

            message(("rs", s, 0, fy), summand_part(2, FIRST), half_in.at[s, 0, fy], zp)
            message(("rs", s, 1, fy), summand_part(2, SECOND), half_in.at[s, 1, fy], zm)
            message(("rs", s, 2, fy), summand(1), full_in.at[s, 0, fy], zp)
            message(("rs", s, 3, fy), summand(3), full_in.at[s, 1, fy], zm)
        message(
            ("rs", s, 4), pbuf.at[s, pl.ds(slot_of(0, 1) * ROWS, ROWS), :], last_in.at[s], yp
        )

    barrier = pltpu.get_barrier_semaphore()
    peers = [sib, ylp, xp, xm] + [at(fh=fy, dz=dz) for dz, fy in others]
    for device in peers:
        pl.semaphore_signal(barrier, inc=1, device_id=device, device_id_type=MESH)

    loads = []

    def load(src, dst):
        copy = pltpu.make_async_copy(src, dst, local_sem.at[len(loads)])
        copy.start()
        loads.append(copy)
        return copy

    load_stale = [
        load(stale_kv.at[:, :, pl.ds(hh * HD, HD)], own_stale.at[:, hh]) for hh in range(2)
    ]
    load_wt = load(text_qkv, wt)
    load_wv = load(video_qkv, wv)
    load_wov = load(video_out_w, wov)
    load_wot = load(text_out_w, wot)

    def normalize_video(s):
        xg[s, 0:ROWS, :] = modulated(
            video_in[s], video_mod[s, 0:1, :], video_mod[s, 1:2, :]
        ).astype(BF16)

    normalize_video(0)
    for s in range(2):
        normed = modulated(text_in[s], text_mod[s, 0:1, :], text_mod[s, 1:2, :])
        for piece in range(4):
            tpack[4 * piece + 2 * s : 4 * piece + 2 * s + 2, :] = normed[
                :, piece * PIECE : (piece + 1) * PIECE
            ]
    tg[0] = tpack[...].astype(BF16)

    pl.semaphore_wait(barrier, len(peers))

    start(("ag", 0, 0), ("ag", 0, 1), ("ag", 0, 2))
    for dz, fy in others:
        start(("ta", dz, fy))
    for copy in load_stale:
        copy.wait()
    start(("kv0", 1), ("kv0", 2), ("kv0", 3), ("kv0", 0))
    normalize_video(1)

    def ag_event(s, number):
        waits, sends = [
            ((0,), (3, 4)),
            ((1, 2), (5, 6)),
            ((3, 4), (7, 8)),
            ((5, 6, 7, 8), ()),
        ][number]
        arrived(*[("ag", s, i) for i in waits])
        start(*[("ag", s, i) for i in sends])

    def project_text():
        arrived(*[("ta", dz, fy) for dz, fy in others])
        packed = tg[...].reshape(128, PIECE)
        for piece in range(4):
            tx[:, piece * PIECE : (piece + 1) * PIECE] = jnp.dot(
                piece_select(piece, False), packed, preferred_element_type=F32
            ).astype(BF16)
        load_wt.wait()
        for j in range(3):
            projected = jnp.dot(tx[...], wt[j], preferred_element_type=F32)
            for hh in range(2):
                one = projected[:, hh * HD : (hh + 1) * HD]
                if j < 2:
                    one = head_norm(one, norm_gains[2 + j : 3 + j, :])
                one = one.astype(BF16)
                if j == 0:
                    for s in range(2):
                        q_ref[s, hh, VID:QROWS, :] = one[s * TXT : (s + 1) * TXT]
                else:
                    tkv[0, j - 1, hh] = one

    def project_video(s):
        for j in range(3):
            projected = jnp.dot(xg[s], wv[j], preferred_element_type=F32)
            for hh in range(2):
                one = projected[:, hh * HD : (hh + 1) * HD]
                if j < 2:
                    one = head_norm(one, norm_gains[j : j + 1, :])
                one = one.astype(BF16)
                if j == 0:
                    q_ref[s, hh, 0:VID, :] = one
                else:
                    kvb[1 - s, 0, j - 1, hh] = one

    def attend(s, block, is_first=False):
        def one_head(hh, carry):
            keys, values = block(0, hh), block(1, hh)
            scores = lax.dot_general(
                q_ref[s, hh], keys, (((1,), (1,)), ((), ())), preferred_element_type=F32
            )
            highest = jnp.max(scores, axis=1, keepdims=True)
            if not is_first:
                before = m_ref[hh][:, 0:1]
                highest = jnp.maximum(highest, before)
            weights = jnp.exp2((scores - highest) * EXP2_SCALE)
            total = jnp.sum(weights, axis=1, keepdims=True)
            mixed = jnp.dot(weights.astype(BF16), values, preferred_element_type=F32)
            if not is_first:
                shrink = jnp.exp2((before - highest) * EXP2_SCALE)
                total = total + l_ref[hh][:, 0:1] * shrink
                mixed = mixed + acc_ref[hh] * shrink
            m_ref[hh] = jnp.broadcast_to(highest, (QROWS, HD))
            l_ref[hh] = jnp.broadcast_to(total, (QROWS, HD))
            acc_ref[hh] = mixed
            return carry

        lax.fori_loop(0, 2, one_head, 0)

    def own_block(s):
        return lambda which, hh: kvb[1 - s, 0, which, hh]

    def text_block(s):
        return lambda which, hh: tkv[:, which, hh, s * TXT : (s + 1) * TXT, :].reshape(16 * TXT, HD)

    def groups(s, low, high):
        return lambda which, hh: kvb[s, low:high, which, hh].reshape((high - low) * VID, HD)

    def finish(s):
        for hh in range(2):
            context = (acc_ref[hh] / l_ref[hh][:, 0:1]).astype(BF16)
            ctx[:, hh * HD : (hh + 1) * HD] = context[0:VID]
            ctxt[s * TXT : (s + 1) * TXT, hh * HD : (hh + 1) * HD] = context[VID:QROWS]
        for tile in range(6):
            cols = slice(tile * 512, (tile + 1) * 512)
            pbuf[s, :, cols] = jnp.dot(
                ctx[...], wov[:, cols], preferred_element_type=F32
            ).astype(BF16)

    def rs_start(s):
        for fy in (1, 0):
            start(("rs", s, 0, fy), ("rs", s, 1, fy))

    def rs_pass(s, fy):
        arrived(("rs", s, 0, fy))
        near = slice(slot_of(1, fy) * ROWS, (slot_of(1, fy) + 1) * ROWS)
        pbuf[s, near, 0:HALF] = (
            pbuf[s, near, 0:HALF].astype(F32) + half_in[s, 0, fy].astype(F32)
        ).astype(BF16)
        start(("rs", s, 2, fy))
        arrived(("rs", s, 1, fy))
        near = slice(slot_of(3, fy) * ROWS, (slot_of(3, fy) + 1) * ROWS)
        pbuf[s, near, HALF:D] = (
            pbuf[s, near, HALF:D].astype(F32) + half_in[s, 1, fy].astype(F32)
        ).astype(BF16)
        start(("rs", s, 3, fy))

    def rs_across(s):
        arrived(("rs", s, 2, 1), ("rs", s, 3, 1))
        mine = slice(slot_of(0, 1) * ROWS, (slot_of(0, 1) + 1) * ROWS)
        pbuf[s, mine, :] = (
            pbuf[s, mine, :].astype(F32)
            + full_in[s, 0, 1].astype(F32)
            + full_in[s, 1, 1].astype(F32)
        ).astype(BF16)
        start(("rs", s, 4))

    def rs_end(s):
        arrived(("rs", s, 2, 0), ("rs", s, 3, 0), ("rs", s, 4))
        summed = (
            pbuf[s, 0:ROWS, :].astype(F32)
            + full_in[s, 0, 0].astype(F32)
            + full_in[s, 1, 0].astype(F32)
            + last_in[s].astype(F32)
        )
        video_out[s] = (video_in[s].astype(F32) + video_mod[s, 2:3, :] * summed).astype(BF16)

    def text_sums():
        load_wot.wait()
        packed = jnp.zeros((128, PIECE), F32)
        for piece in range(4):
            term = jnp.dot(
                ctxt[...],
                wot[:, piece * PIECE : (piece + 1) * PIECE],
                preferred_element_type=F32,
            ).astype(BF16)
            packed = packed + jnp.dot(
                piece_select(piece, True), term, preferred_element_type=F32
            )
        tp[...] = packed.astype(BF16).reshape(8, 16, PIECE)
        for dz, fy in others:
            start(("tr", dz, fy))

    def text_end():
        arrived(*[("tr", dz, fy) for dz, fy in others])
        summed = tp[0].astype(F32)
        for dz, fy in others:
            summed = summed + trx[slot_of(dz, fy)].astype(F32)
        tpack[...] = summed
        for s in range(2):
            rows = jnp.concatenate(
                [tpack[4 * i + 2 * s : 4 * i + 2 * s + 2, :] for i in range(4)], axis=1
            )
            text_out[s] = (text_in[s].astype(F32) + text_mod[s, 2:3, :] * rows).astype(BF16)

    def store_fresh():
        copies = []
        for dz in range(4):
            for fy in range(2):
                slot = slot_of(dz, fy)
                owner_y = 1 - yh if fy else yh
                owner = owner_y * 4 + (z + dz) % 4
                place = pl.ds(pl.multiple_of(owner * ROWS, ROWS), ROWS)
                for hh in range(2):
                    copy = pltpu.make_async_copy(
                        kvb.at[0, 0, :, hh, pl.ds(slot * ROWS, ROWS), :],
                        fresh_kv.at[:, place, pl.ds(hh * HD, HD)],
                        out_sem.at[slot * 2 + hh],
                    )
                    copy.start()
                    copies.append(copy)
        return copies

    ag_event(0, 0)
    ag_event(0, 1)
    project_text()
    start(("tkv", 1), ("tkv", 2), ("tkv", 3), ("tkv", 0))
    patch_event("kv0", 0)
    ag_event(0, 2)
    patch_event("kv0", 1)
    start(("ag", 1, 0), ("ag", 1, 1), ("ag", 1, 2))
    patch_event("tkv", 0)
    patch_event("tkv", 1)
    load_wv.wait()
    ag_event(0, 3)
    project_video(0)
    start(("kv1", 1), ("kv1", 2), ("kv1", 3), ("kv1", 0))
    patch_event("kv0", 2)
    patch_event("tkv", 2)
    attend(0, own_block(0), True)
    ag_event(1, 0)
    ag_event(1, 1)
    patch_event("tkv", 3)
    patch_event("tkv", 4)
    arrived(("kv0", 0), ("kv0", 4))
    attend(0, groups(0, 1, 4))
    patch_event("kv0", 3)
    patch_event("kv0", 4)
    patch_event("kv1", 0)
    patch_event("kv1", 1)
    arrived(("kv0", 9), ("kv0", 13))
    attend(0, groups(0, 4, 8))
    ag_event(1, 2)
    arrived(("kv0", 7), ("kv0", 11))
    attend(0, groups(0, 12, 16))
    arrived(*[("tkv", i) for i in (0, 4, 7, 9, 11, 13, 15, 16)])
    attend(0, text_block(0))
    arrived(("kv0", 15), ("kv0", 16))
    attend(0, groups(0, 8, 12))
    load_wov.wait()
    finish(0)
    patch_event("kv1", 2)
    ag_event(1, 3)
    rs_start(0)
    project_video(1)
    fresh_copies = store_fresh()
    rs_pass(0, 1)
    rs_pass(0, 0)
    attend(1, own_block(1), True)
    patch_event("kv1", 3)
    patch_event("kv1", 4)
    attend(1, text_block(1))
    rs_across(0)
    arrived(("kv1", 0), ("kv1", 4))
    attend(1, groups(1, 1, 4))
    arrived(("kv1", 9), ("kv1", 13))
    attend(1, groups(1, 4, 8))
    arrived(("kv1", 7), ("kv1", 11))
    attend(1, groups(1, 12, 16))
    arrived(("kv1", 15), ("kv1", 16))
    attend(1, groups(1, 8, 12))
    finish(1)
    rs_start(1)
    text_sums()
    rs_end(0)
    rs_pass(1, 1)
    rs_pass(1, 0)
    rs_across(1)
    text_end()
    rs_end(1)
    for copy in fresh_copies:
        copy.wait()
    for make in table.values():
        make().wait_send()


def shards(*arrays):
    vmem = pl.BlockSpec(memory_space=pltpu.VMEM)
    hbm = pl.BlockSpec(memory_space=pl.ANY)
    scratch = [
        pltpu.VMEM((3, D, 256), BF16),
        pltpu.VMEM((3, D, 256), BF16),
        pltpu.VMEM((256, D), BF16),
        pltpu.VMEM((256, D), BF16),
        pltpu.VMEM((2, VID, D), BF16),
        pltpu.VMEM((16, PIECE), F32),
        pltpu.VMEM((8, 16, PIECE), BF16),
        pltpu.VMEM((32, D), BF16),
        pltpu.VMEM((2, 2, QROWS, HD), BF16),
        pltpu.VMEM((2, 2, VID, HD), BF16),
        pltpu.VMEM((2, 16, 2, 2, VID, HD), BF16),
        pltpu.VMEM((16, 2, 2, 2 * TXT, HD), BF16),
        pltpu.VMEM((2, QROWS, HD), F32),
        pltpu.VMEM((2, QROWS, HD), F32),
        pltpu.VMEM((2, QROWS, HD), F32),
        pltpu.VMEM((VID, 256), BF16),
        pltpu.VMEM((2 * TXT, 256), BF16),
        pltpu.VMEM((2, VID, D), BF16),
        pltpu.VMEM((2, 2, 2, ROWS, HALF), BF16),
        pltpu.VMEM((2, 2, 2, ROWS, D), BF16),
        pltpu.VMEM((2, ROWS, D), BF16),
        pltpu.VMEM((8, 16, PIECE), BF16),
        pltpu.VMEM((8, 16, PIECE), BF16),
        pltpu.SemaphoreType.DMA((101,)),
        pltpu.SemaphoreType.DMA((101,)),
        pltpu.SemaphoreType.DMA((6,)),
        pltpu.SemaphoreType.DMA((16,)),
    ]
    return pl.pallas_call(
        kernel,
        out_shape=(
            jax.ShapeDtypeStruct((2, ROWS, D), BF16),
            jax.ShapeDtypeStruct((2, 2, D), BF16),
            jax.ShapeDtypeStruct((2, VID, 256), BF16),
        ),
        in_specs=[vmem, vmem, vmem, vmem, hbm, hbm, hbm, hbm, vmem, hbm],
        out_specs=(vmem, vmem, hbm),
        scratch_shapes=scratch,
        compiler_params=pltpu.CompilerParams(
            collective_id=0, has_side_effects=True, vmem_limit_bytes=56 * 1024 * 1024
        ),
        cost_estimate=pl.CostEstimate(
            flops=6_000_000_000, bytes_accessed=16_000_000, transcendentals=4_800_000
        ),
    )(*arrays)


def solution(mesh):
    return jax.shard_map(
        shards,
        mesh=mesh,
        in_specs=(
            P(None, ("patch", "head"), None),
            P(None, ("patch", "head"), None),
            P(),
            P(),
            P(None, None, "head"),
            P(None, None, "head"),
            P("head", None),
            P("head", None),
            P(),
            P(None, "patch", "head"),
        ),
        out_specs=(
            P(None, ("patch", "head"), None),
            P(None, ("patch", "head"), None),
            P(None, "patch", "head"),
        ),
        check_vma=False,
    )
```

time: 329 us -> 100 us (0.30)
  waiting for transfers between devices: 111 us -> 0 us
  Pallas kernels: 0 us -> 91.3 us
  blocking collectives: 88.5 us -> 0 us
  matrix products: 37.4 us -> 0 us
  local copies, waits for them, and re-layouts: 38.7 us -> 7.92 us
  other arithmetic: 21 us -> 0 us
  starting transfers between devices: 14.9 us -> 0 us
  between operations: 15.4 us -> 0.64 us
    all_gather x4 -> x0, waiting for transfers between devices: 111 us -> none  [the longest x2 98.3 us: prepare(): gathered = lax.all_gather(local_rows, 'head', axis=0, tiled=True)]
    pallas_call x0 -> x1, Pallas kernels: none -> 91.3 us  [shards(): pl.pallas_call(kernel, out_shape=(jax.ShapeDtypeStruct((2, ROWS, D), BF16...]
    unnamed x1 -> x0, blocking collectives: 51.6 us -> none
    dot_general x20 -> x0, matrix products: 37.4 us -> none  [the longest x4 14.8 us: project(): jnp.einsum('rd,jdc->jrc', normed, weights, preferred_element_type=jnp.flo...]
    all_gather x2 -> x0, blocking collectives: 36.9 us -> none  [gather_text(): return lax.all_gather(fresh_text, 'patch', axis=1, tiled=True)]
    unnamed x4 -> x0, starting transfers between devices: 14.8 us -> none
    slice x22 -> x0, local copies, waits for them, and re-layouts: 12.5 us -> none  [the longest x2 2.86 us: prepare(): text_part = blocks[:, video_count:].reshape(-1, blocks.shape[2])]
    reduce_sum x17 -> x0, other arithmetic: 8.14 us -> none  [the longest x5 3.18 us: fold_block(): running_sum = running_sum * shrink + jnp.sum(weights, axis=2)]
  transfers between devices with their start and end apart: 8 -> 0, of which waited for: 3 -> 0; matrix products, arithmetic and copies ran while one was open for 16% -> 0% of each run, Pallas kernels for 0% -> 0%
where the time goes in v1:
time: 100 us; the launch traced here: 99.8 us
  Pallas kernels  91.3 us (91%)
  local copies, waits for them, and re-layouts  7.92 us (8%)
    pallas_call x1, Pallas kernels, shards(): pl.pallas_call(kernel, out_shape=(jax.ShapeDtypeStruct((2, ROWS, D), BF16...  91.3 us
    unnamed x5, local copies, waits for them, and re-layouts  7.92 us

profile of v1, /device:TPU:0, one launch (start us, length us, event | category | flops | bytes accessed | tf_op | source)
XLA Modules:
  0.0 99.8 jit_solution(2987573307347605032)
XLA Ops:
  0.6 1.6 %copy.13.video_mod = f32[2,3,3072]{2,1,0:T(4,128)} copy(f32[2,3,3072]{2,0,1:T(2,128)} %param.12) | data formatting | bytes 147456 | tf_op args[2]
  2.2 1.6 %copy.14.text_mod = f32[2,3,3072]{2,1,0:T(4,128)} copy(f32[2,3,3072]{2,0,1:T(2,128)} %param.13) | data formatting | bytes 147456 | tf_op args[3]
  3.8 91.3 %shard_map.121 = (bf16[2,32,3072]{2,1,0:T(8,128)(2,1)}, bf16[2,2,3072]{2,1,0:T(2,128)(2,1)}, bf16[2,256,256]{2,1,0:T(8,128)(2,1)}) custom-call(bf16[2,32,3072]{2,1,0:T(8,128)(2,1)} %video_in.1, bf16[2,2,3072]{2,1,0:T(2,128)(2,1)} %text_in.1, f32[2,3,3072]{2,1,0:T(4,128)} %copy.13.video_mod, f32[2,3,3072]{2,1,0:T(4,128)} %copy.14.text_mod, ...), custom_call_target="tpu_custom_call" | custom-call | flops 6000000000 | bytes 16000000 | tf_op jit(solution)/shard_map/pallas_call | solution.py:540
  95.0 1.8 %copy.18 = bf16[2,32,3072]{2,1,0:T(8,128)(2,1)} copy(bf16[2,32,3072]{2,1,0:T(8,128)(2,1)} %get-tuple-element.6) | data formatting | bytes 786432
  96.8 1.4 %copy.19 = bf16[2,2,3072]{2,1,0:T(2,128)(2,1)} copy(bf16[2,2,3072]{2,1,0:T(2,128)(2,1)} %get-tuple-element.7) | data formatting | bytes 49152
  98.2 1.7 %copy.20 = bf16[2,256,256]{2,1,0:T(8,128)(2,1)} copy(bf16[2,256,256]{2,1,0:T(8,128)(2,1)} %get-tuple-element.8) | data formatting | bytes 524288

commit v2 on v1

--- a/solution.py
+++ b/solution.py
@@ -50,8 +50,8 @@
     return (dz % 4) * 2 + fy
 
 
-def group_of(dx, fy, fc):
-    return (dx % 4) * 4 + fy * 2 + fc
+def group_of(dx, fc):
+    return (dx % 4) * 2 + fc
 
 
 def kernel(
@@ -77,12 +77,19 @@
     tg,
     tx,
     q_ref,
-    own_stale,
+    q_peer,
     kvb,
+    fresh,
     tkv,
     m_ref,
     l_ref,
     acc_ref,
+    stat,
+    stat_t,
+    part_out,
+    part_in,
+    stat_out,
+    stat_in,
     ctx,
     ctxt,
     pbuf,
@@ -154,42 +161,30 @@
         message(("ag", s, 7), part(3, 1, FIRST), part(2, 1, FIRST), zp)
         message(("ag", s, 8), part(1, 1, SECOND), part(2, 1, SECOND), zm)
 
-    def gather_patch(kind, own, block):
-        def half(dx, fy, which):
-            return block(dx, fy, 0).at[which]
-
-        message((kind, 0), own, block(0, 0, 1), sib)
-        message((kind, 1), own, block(0, 1, 0), ylp)
-        message((kind, 2), own, block(3, 0, 0), xp)
-        message((kind, 3), own, block(1, 0, 0), xm)
-        message((kind, 4), block(0, 1, 0), block(0, 1, 1), sib)
-        message((kind, 5), block(0, 1, 0), block(3, 1, 0), xp)
-        message((kind, 6), block(0, 1, 0), block(1, 1, 0), xm)
-        message((kind, 7), block(3, 0, 0), block(3, 0, 1), sib)
-        message((kind, 8), half(3, 0, 0), half(2, 0, 0), xp)
-        message((kind, 9), block(1, 0, 0), block(1, 0, 1), sib)
-        message((kind, 10), half(1, 0, 1), half(2, 0, 1), xm)
-        message((kind, 11), block(3, 1, 0), block(3, 1, 1), sib)
-        message((kind, 12), half(3, 1, 0), half(2, 1, 0), xp)
-        message((kind, 13), block(1, 1, 0), block(1, 1, 1), sib)
-        message((kind, 14), half(1, 1, 1), half(2, 1, 1), xm)
-        message((kind, 15), block(2, 0, 0), block(2, 0, 1), sib)
-        message((kind, 16), block(2, 1, 0), block(2, 1, 1), sib)
-
-    gather_patch("kv0", own_stale, lambda dx, fy, fc: kvb.at[0, group_of(dx, fy, fc)])
-    gather_patch("kv1", kvb.at[1, 0], lambda dx, fy, fc: kvb.at[1, group_of(dx, fy, fc)])
-    gather_patch("tkv", tkv.at[0], lambda dx, fy, fc: tkv.at[group_of(dx, fy, fc)])
-
-    def patch_event(kind, number):
-        waits, sends = [
-            ((1,), (5, 6, 4)),
-            ((2, 3), (8, 10, 7, 9)),
-            ((5, 6), (12, 14, 11, 13)),
-            ((8, 10), (15,)),
-            ((12, 14), (16,)),
-        ][number]
+    def gather_x(kind, block):
+        message((kind, 0), block(0, 0), block(0, 1), sib)
+        message((kind, 1), block(0, 0), block(3, 0), xp)
+        message((kind, 2), block(0, 0), block(1, 0), xm)
+        message((kind, 3), block(3, 0), block(3, 1), sib)
+        message((kind, 4), block(3, 0).at[0], block(2, 0).at[0], xp)
+        message((kind, 5), block(1, 0), block(1, 1), sib)
+        message((kind, 6), block(1, 0).at[1], block(2, 0).at[1], xm)
+        message((kind, 7), block(2, 0), block(2, 1), sib)
+
+    gather_x("kv0", lambda dx, fc: kvb.at[0, group_of(dx, fc)])
+    gather_x("kv1", lambda dx, fc: kvb.at[1, group_of(dx, fc)])
+    gather_x("tkv", lambda dx, fc: tkv.at[group_of(dx, fc)])
+
+    def x_event(kind, number):
+        waits, sends = [((1, 2), (4, 6, 3, 5)), ((4, 6), (7,))][number]
         arrived(*[(kind, i) for i in waits])
         start(*[(kind, i) for i in sends])
+
+    for s in range(2):
+        for hh in range(2):
+            message(("q", s, hh), q_ref.at[s, hh], q_peer.at[s, hh], ylp)
+            message(("pc", s, hh), part_out.at[s, hh], part_in.at[s, hh], ylp)
+            message(("st", s, hh), stat_out.at[s, hh], stat_in.at[s, hh], ylp)
 
     others = [(dz, fy) for dz in range(4) for fy in range(2) if (dz, fy) != (0, 0)]
     for dz, fy in others:
@@ -229,7 +224,7 @@
         return copy
 
     load_stale = [
-        load(stale_kv.at[:, :, pl.ds(hh * HD, HD)], own_stale.at[:, hh]) for hh in range(2)
+        load(stale_kv.at[:, :, pl.ds(hh * HD, HD)], kvb.at[0, 0, :, hh]) for hh in range(2)
     ]
     load_wt = load(text_qkv, wt)
     load_wv = load(video_qkv, wv)
@@ -238,12 +233,12 @@
 
     def normalize_video(s):
         xg[s, 0:ROWS, :] = modulated(
-            video_in[s], video_mod[s, 0:1, :], video_mod[s, 1:2, :]
+            video_in[s], video_mod[0, s : s + 1, :], video_mod[1, s : s + 1, :]
         ).astype(BF16)
 
     normalize_video(0)
     for s in range(2):
-        normed = modulated(text_in[s], text_mod[s, 0:1, :], text_mod[s, 1:2, :])
+        normed = modulated(text_in[s], text_mod[0, s : s + 1, :], text_mod[1, s : s + 1, :])
         for piece in range(4):
             tpack[4 * piece + 2 * s : 4 * piece + 2 * s + 2, :] = normed[
                 :, piece * PIECE : (piece + 1) * PIECE
@@ -257,7 +252,7 @@
         start(("ta", dz, fy))
     for copy in load_stale:
         copy.wait()
-    start(("kv0", 1), ("kv0", 2), ("kv0", 3), ("kv0", 0))
+    start(("kv0", 1), ("kv0", 2), ("kv0", 0))
     normalize_video(1)
 
     def ag_event(s, number):
@@ -291,57 +286,75 @@
                 else:
                     tkv[0, j - 1, hh] = one
 
-    def project_video(s):
-        for j in range(3):
-            projected = jnp.dot(xg[s], wv[j], preferred_element_type=F32)
-            for hh in range(2):
-                one = projected[:, hh * HD : (hh + 1) * HD]
-                if j < 2:
-                    one = head_norm(one, norm_gains[j : j + 1, :])
-                one = one.astype(BF16)
-                if j == 0:
-                    q_ref[s, hh, 0:VID, :] = one
-                else:
-                    kvb[1 - s, 0, j - 1, hh] = one
-
-    def attend(s, block, is_first=False):
-        def one_head(hh, carry):
-            keys, values = block(0, hh), block(1, hh)
-            scores = lax.dot_general(
-                q_ref[s, hh], keys, (((1,), (1,)), ((), ())), preferred_element_type=F32
-            )
-            highest = jnp.max(scores, axis=1, keepdims=True)
-            if not is_first:
-                before = m_ref[hh][:, 0:1]
-                highest = jnp.maximum(highest, before)
-            weights = jnp.exp2((scores - highest) * EXP2_SCALE)
-            total = jnp.sum(weights, axis=1, keepdims=True)
-            mixed = jnp.dot(weights.astype(BF16), values, preferred_element_type=F32)
-            if not is_first:
-                shrink = jnp.exp2((before - highest) * EXP2_SCALE)
-                total = total + l_ref[hh][:, 0:1] * shrink
-                mixed = mixed + acc_ref[hh] * shrink
-            m_ref[hh] = jnp.broadcast_to(highest, (QROWS, HD))
-            l_ref[hh] = jnp.broadcast_to(total, (QROWS, HD))
-            acc_ref[hh] = mixed
-            return carry
-
-        lax.fori_loop(0, 2, one_head, 0)
+    def project_video(s, j):
+        projected = jnp.dot(xg[s], wv[j], preferred_element_type=F32)
+        for hh in range(2):
+            one = projected[:, hh * HD : (hh + 1) * HD]
+            if j < 2:
+                one = head_norm(one, norm_gains[j : j + 1, :])
+            one = one.astype(BF16)
+            if j == 0:
+                q_ref[s, hh, 0:VID, :] = one
+            elif s == 0:
+                kvb[1, 0, j - 1, hh] = one
+            else:
+                fresh[j - 1, hh] = one
 
     def own_block(s):
-        return lambda which, hh: kvb[1 - s, 0, which, hh]
+        return lambda which, hh: kvb[1, 0, which, hh] if s == 0 else fresh[which, hh]
 
     def text_block(s):
-        return lambda which, hh: tkv[:, which, hh, s * TXT : (s + 1) * TXT, :].reshape(16 * TXT, HD)
+        return lambda which, hh: tkv[:, which, hh, s * TXT : (s + 1) * TXT, :].reshape(8 * TXT, HD)
 
     def groups(s, low, high):
         return lambda which, hh: kvb[s, low:high, which, hh].reshape((high - low) * VID, HD)
 
+    def attend(s, who, hh, blocks, is_first=False):
+        keys = jnp.concatenate([block(0, hh) for block in blocks], axis=0)
+        values = jnp.concatenate([block(1, hh) for block in blocks], axis=0)
+        queries = q_peer[s, hh] if who else q_ref[s, hh]
+        scores = lax.dot_general(
+            queries, keys, (((1,), (1,)), ((), ())), preferred_element_type=F32
+        )
+        highest = jnp.max(scores, axis=1, keepdims=True)
+        if not is_first:
+            before = m_ref[who, hh][:, 0:1]
+            highest = jnp.maximum(highest, before)
+        weights = jnp.exp2((scores - highest) * EXP2_SCALE)
+        total = jnp.sum(weights, axis=1, keepdims=True)
+        mixed = jnp.dot(weights.astype(BF16), values, preferred_element_type=F32)
+        if not is_first:
+            shrink = jnp.exp2((before - highest) * EXP2_SCALE)
+            total = total + l_ref[who, hh][:, 0:1] * shrink
+            mixed = mixed + acc_ref[who, hh] * shrink
+        m_ref[who, hh] = jnp.broadcast_to(highest, (QROWS, HD))
+        l_ref[who, hh] = jnp.broadcast_to(total, (QROWS, HD))
+        acc_ref[who, hh] = mixed
+
+    def give_back(s, hh):
+        part_out[s, hh] = (acc_ref[1, hh] / l_ref[1, hh][:, 0:1]).astype(BF16)
+        lane = lax.broadcasted_iota(jnp.int32, (QROWS, HD), 1)
+        stat[0:QROWS, :] = jnp.where(lane == 0, m_ref[1, hh], l_ref[1, hh])
+        stat_out[s, hh] = jnp.transpose(stat[...])[0:8, :]
+        start(("pc", s, hh), ("st", s, hh))
+
+    def merge(s, hh):
+        arrived(("pc", s, hh), ("st", s, hh))
+        stat_t[0:8, :] = stat_in[s, hh]
+        theirs = jnp.transpose(stat_t[...])[0:QROWS, :]
+        m_there, l_there = theirs[:, 0:1], theirs[:, 1:2]
+        m_here, l_here = m_ref[0, hh][:, 0:1], l_ref[0, hh][:, 0:1]
+        highest = jnp.maximum(m_here, m_there)
+        here = jnp.exp2((m_here - highest) * EXP2_SCALE)
+        there = jnp.exp2((m_there - highest) * EXP2_SCALE) * l_there
+        context = (acc_ref[0, hh] * here + part_in[s, hh].astype(F32) * there) / (
+            l_here * here + there
+        )
+        context = context.astype(BF16)
+        ctx[:, hh * HD : (hh + 1) * HD] = context[0:VID]
+        ctxt[s * TXT : (s + 1) * TXT, hh * HD : (hh + 1) * HD] = context[VID:QROWS]
+
     def finish(s):
-        for hh in range(2):
-            context = (acc_ref[hh] / l_ref[hh][:, 0:1]).astype(BF16)
-            ctx[:, hh * HD : (hh + 1) * HD] = context[0:VID]
-            ctxt[s * TXT : (s + 1) * TXT, hh * HD : (hh + 1) * HD] = context[VID:QROWS]
         for tile in range(6):
             cols = slice(tile * 512, (tile + 1) * 512)
             pbuf[s, :, cols] = jnp.dot(
@@ -384,7 +397,7 @@
             + full_in[s, 1, 0].astype(F32)
             + last_in[s].astype(F32)
         )
-        video_out[s] = (video_in[s].astype(F32) + video_mod[s, 2:3, :] * summed).astype(BF16)
+        video_out[s] = (video_in[s].astype(F32) + video_mod[2, s : s + 1, :] * summed).astype(BF16)
 
     def text_sums():
         load_wot.wait()
@@ -412,7 +425,7 @@
             rows = jnp.concatenate(
                 [tpack[4 * i + 2 * s : 4 * i + 2 * s + 2, :] for i in range(4)], axis=1
             )
-            text_out[s] = (text_in[s].astype(F32) + text_mod[s, 2:3, :] * rows).astype(BF16)
+            text_out[s] = (text_in[s].astype(F32) + text_mod[2, s : s + 1, :] * rows).astype(BF16)
 
     def store_fresh():
         copies = []
@@ -424,7 +437,7 @@
                 place = pl.ds(pl.multiple_of(owner * ROWS, ROWS), ROWS)
                 for hh in range(2):
                     copy = pltpu.make_async_copy(
-                        kvb.at[0, 0, :, hh, pl.ds(slot * ROWS, ROWS), :],
+                        fresh.at[:, hh, pl.ds(slot * ROWS, ROWS), :],
                         fresh_kv.at[:, place, pl.ds(hh * HD, HD)],
                         out_sem.at[slot * 2 + hh],
                     )
@@ -433,63 +446,71 @@
         return copies
 
     ag_event(0, 0)
+    start(("ag", 1, 0))
     ag_event(0, 1)
     project_text()
-    start(("tkv", 1), ("tkv", 2), ("tkv", 3), ("tkv", 0))
-    patch_event("kv0", 0)
+    start(("tkv", 1), ("tkv", 2), ("tkv", 0))
+    x_event("kv0", 0)
     ag_event(0, 2)
-    patch_event("kv0", 1)
-    start(("ag", 1, 0), ("ag", 1, 1), ("ag", 1, 2))
-    patch_event("tkv", 0)
-    patch_event("tkv", 1)
+    start(("ag", 1, 1), ("ag", 1, 2))
+    x_event("tkv", 0)
+    ag_event(1, 0)
+    x_event("kv0", 1)
+    x_event("tkv", 1)
     load_wv.wait()
     ag_event(0, 3)
-    project_video(0)
-    start(("kv1", 1), ("kv1", 2), ("kv1", 3), ("kv1", 0))
-    patch_event("kv0", 2)
-    patch_event("tkv", 2)
-    attend(0, own_block(0), True)
-    ag_event(1, 0)
+    project_video(0, 0)
+    start(("q", 0, 0), ("q", 0, 1))
+    project_video(0, 1)
+    project_video(0, 2)
+    start(("kv1", 1), ("kv1", 2), ("kv1", 0))
+    arrived(*[("tkv", i) for i in (0, 3, 5, 7)])
+    for hh in range(2):
+        attend(0, 0, hh, [own_block(0), text_block(0)], True)
+    arrived(("kv0", 0), ("kv0", 5))
     ag_event(1, 1)
-    patch_event("tkv", 3)
-    patch_event("tkv", 4)
-    arrived(("kv0", 0), ("kv0", 4))
-    attend(0, groups(0, 1, 4))
-    patch_event("kv0", 3)
-    patch_event("kv0", 4)
-    patch_event("kv1", 0)
-    patch_event("kv1", 1)
-    arrived(("kv0", 9), ("kv0", 13))
-    attend(0, groups(0, 4, 8))
+    for hh in range(2):
+        attend(0, 0, hh, [groups(0, 1, 4)])
+    arrived(("kv0", 3), ("kv0", 7))
+    for hh in range(2):
+        arrived(("q", 0, hh))
+        attend(0, 1, hh, [groups(0, 0, 4)], True)
+        attend(0, 1, hh, [groups(0, 4, 8), text_block(0)])
+        give_back(0, hh)
     ag_event(1, 2)
-    arrived(("kv0", 7), ("kv0", 11))
-    attend(0, groups(0, 12, 16))
-    arrived(*[("tkv", i) for i in (0, 4, 7, 9, 11, 13, 15, 16)])
-    attend(0, text_block(0))
-    arrived(("kv0", 15), ("kv0", 16))
-    attend(0, groups(0, 8, 12))
+    x_event("kv1", 0)
+    for hh in range(2):
+        attend(0, 0, hh, [groups(0, 4, 8)])
     load_wov.wait()
+    for hh in range(2):
+        merge(0, hh)
     finish(0)
-    patch_event("kv1", 2)
+    rs_start(0)
+    x_event("kv1", 1)
     ag_event(1, 3)
-    rs_start(0)
-    project_video(1)
+    project_video(1, 0)
+    start(("q", 1, 0), ("q", 1, 1))
+    project_video(1, 1)
+    project_video(1, 2)
     fresh_copies = store_fresh()
     rs_pass(0, 1)
     rs_pass(0, 0)
-    attend(1, own_block(1), True)
-    patch_event("kv1", 3)
-    patch_event("kv1", 4)
-    attend(1, text_block(1))
+    for hh in range(2):
+        attend(1, 0, hh, [own_block(1), text_block(1)], True)
+    arrived(("kv1", 0), ("kv1", 5))
+    for hh in range(2):
+        attend(1, 0, hh, [groups(1, 1, 4)])
+    arrived(("kv1", 3), ("kv1", 7))
     rs_across(0)
-    arrived(("kv1", 0), ("kv1", 4))
-    attend(1, groups(1, 1, 4))
-    arrived(("kv1", 9), ("kv1", 13))
-    attend(1, groups(1, 4, 8))
-    arrived(("kv1", 7), ("kv1", 11))
-    attend(1, groups(1, 12, 16))
-    arrived(("kv1", 15), ("kv1", 16))
-    attend(1, groups(1, 8, 12))
+    for hh in range(2):
+        arrived(("q", 1, hh))
+        attend(1, 1, hh, [groups(1, 0, 4)], True)
+        attend(1, 1, hh, [groups(1, 4, 8), text_block(1)])
+        give_back(1, hh)
+    for hh in range(2):
+        attend(1, 0, hh, [groups(1, 4, 8)])
+    for hh in range(2):
+        merge(1, hh)
     finish(1)
     rs_start(1)
     text_sums()
@@ -505,6 +526,18 @@
         make().wait_send()
 
 
+def hand_over(*refs):
+    sources, targets, sem = refs[:3], refs[3:6], refs[6]
+    copies = [
+        pltpu.make_async_copy(source, target, sem.at[i])
+        for i, (source, target) in enumerate(zip(sources, targets))
+    ]
+    for copy in copies:
+        copy.start()
+    for copy in copies:
+        copy.wait()
+
+
 def shards(*arrays):
     vmem = pl.BlockSpec(memory_space=pltpu.VMEM)
     hbm = pl.BlockSpec(memory_space=pl.ANY)
@@ -518,12 +551,19 @@
         pltpu.VMEM((8, 16, PIECE), BF16),
         pltpu.VMEM((32, D), BF16),
         pltpu.VMEM((2, 2, QROWS, HD), BF16),
+        pltpu.VMEM((2, 2, QROWS, HD), BF16),
+        pltpu.VMEM((2, 8, 2, 2, VID, HD), BF16),
         pltpu.VMEM((2, 2, VID, HD), BF16),
-        pltpu.VMEM((2, 16, 2, 2, VID, HD), BF16),
-        pltpu.VMEM((16, 2, 2, 2 * TXT, HD), BF16),
-        pltpu.VMEM((2, QROWS, HD), F32),
-        pltpu.VMEM((2, QROWS, HD), F32),
-        pltpu.VMEM((2, QROWS, HD), F32),
+        pltpu.VMEM((8, 2, 2, 2 * TXT, HD), BF16),
+        pltpu.VMEM((2, 2, QROWS, HD), F32),
+        pltpu.VMEM((2, 2, QROWS, HD), F32),
+        pltpu.VMEM((2, 2, QROWS, HD), F32),
+        pltpu.VMEM((384, 128), F32),
+        pltpu.VMEM((128, 384), F32),
+        pltpu.VMEM((2, 2, QROWS, HD), BF16),
+        pltpu.VMEM((2, 2, QROWS, HD), BF16),
+        pltpu.VMEM((2, 2, 8, 384), F32),
+        pltpu.VMEM((2, 2, 8, 384), F32),
         pltpu.VMEM((VID, 256), BF16),
         pltpu.VMEM((2 * TXT, 256), BF16),
         pltpu.VMEM((2, VID, D), BF16),
@@ -532,18 +572,22 @@
         pltpu.VMEM((2, ROWS, D), BF16),
         pltpu.VMEM((8, 16, PIECE), BF16),
         pltpu.VMEM((8, 16, PIECE), BF16),
-        pltpu.SemaphoreType.DMA((101,)),
-        pltpu.SemaphoreType.DMA((101,)),
+        pltpu.SemaphoreType.DMA((86,)),
+        pltpu.SemaphoreType.DMA((86,)),
         pltpu.SemaphoreType.DMA((6,)),
         pltpu.SemaphoreType.DMA((16,)),
     ]
-    return pl.pallas_call(
+    out_shape = (
+        jax.ShapeDtypeStruct((2, ROWS, D), BF16),
+        jax.ShapeDtypeStruct((2, 2, D), BF16),
+        jax.ShapeDtypeStruct((2, VID, 256), BF16),
+    )
+    arrays = list(arrays)
+    arrays[2] = jnp.transpose(arrays[2], (1, 0, 2))
+    arrays[3] = jnp.transpose(arrays[3], (1, 0, 2))
+    finished = pl.pallas_call(
         kernel,
-        out_shape=(
-            jax.ShapeDtypeStruct((2, ROWS, D), BF16),
-            jax.ShapeDtypeStruct((2, 2, D), BF16),
-            jax.ShapeDtypeStruct((2, VID, 256), BF16),
-        ),
+        out_shape=out_shape,
         in_specs=[vmem, vmem, vmem, vmem, hbm, hbm, hbm, hbm, vmem, hbm],
         out_specs=(vmem, vmem, hbm),
         scratch_shapes=scratch,
@@ -554,6 +598,13 @@
             flops=6_000_000_000, bytes_accessed=16_000_000, transcendentals=4_800_000
         ),
     )(*arrays)
+    return pl.pallas_call(
+        hand_over,
+        out_shape=out_shape,
+        in_specs=[hbm] * 3,
+        out_specs=(hbm,) * 3,
+        scratch_shapes=[pltpu.SemaphoreType.DMA((3,))],
+    )(*finished)
 
 
 def solution(mesh):

time: 100 us -> 101 us (1.010)
  Pallas kernels: 91.3 us -> 100 us
  local copies, waits for them, and re-layouts: 7.92 us -> 0 us
    pallas_call x1 -> x2, Pallas kernels: 91.3 us -> 100 us  [the longest x1 78.3 us: shards(): pl.pallas_call(kernel, out_shape=out_shape, in_specs=[vmem, vmem, vmem, v...]
    unnamed x5 -> x0, local copies, waits for them, and re-layouts: 7.92 us -> none
where the time goes in v2:
time: 101 us
  Pallas kernels  100 us (99%)
    pallas_call x1, Pallas kernels, shards(): pl.pallas_call(kernel, out_shape=out_shape, in_specs=[vmem, vmem, vmem, v...  78.3 us
    pallas_call x1, Pallas kernels, shards(): pl.pallas_call(hand_over, out_shape=out_shape, in_specs=[hbm] * 3, out_sp...  21.7 us

profile of v2, /device:TPU:0, one launch (start us, length us, event | category | flops | bytes accessed | tf_op | source)
XLA Modules:
  0.0 100.9 jit_solution(1486963370789376868)
XLA Ops:
  0.6 78.3 %shard_map.121 = (bf16[2,32,3072]{2,1,0:T(8,128)(2,1)}, bf16[2,2,3072]{2,1,0:T(2,128)(2,1)}, bf16[2,256,256]{2,1,0:T(8,128)(2,1)}) custom-call(bf16[2,32,3072]{2,1,0:T(8,128)(2,1)} %video_in.1, bf16[2,2,3072]{2,1,0:T(2,128)(2,1)} %text_in.1, f32[3,2,3072]{2,1,0:T(2,128)} %bitcast.2, f32[3,2,3072]{2,1,0:T(2,128)} %bitcast.3, bf16[3,3072,256]{2,1,0:T(8,128)(2,1)} %video_qkv.1, ...), custom_call_target="tpu_custom_call" | custom-call | flops 6000000000 | bytes 16000000 | tf_op jit(solution)/shard_map/pallas_call | solution.py:588
  79.0 21.7 %shard_map.122 = (bf16[2,32,3072]{2,1,0:T(8,128)(2,1)}, bf16[2,2,3072]{2,1,0:T(2,128)(2,1)}, bf16[2,256,256]{2,1,0:T(8,128)(2,1)}) custom-call(bf16[2,32,3072]{2,1,0:T(8,128)(2,1)} %get-tuple-element.6.refs_0_, bf16[2,2,3072]{2,1,0:T(2,128)(2,1)} %get-tuple-element.7.refs_1_, bf16[2,256,256]{2,1,0:T(8,128)(2,1)} %get-tuple-element.8.refs_2_), custom_call_target="tpu_custom_call" | custom-call | tf_op jit(solution)/shard_map/pallas_call | solution.py:601

commit v3 on v2

--- a/solution.py
+++ b/solution.py
@@ -22,6 +22,7 @@
 QROWS = VID + TXT
 PIECE = 768
 
+NEAR = 2048
 FIRST, SECOND = pl.ds(0, HALF), pl.ds(HALF, HALF)
 
 
@@ -70,7 +71,7 @@
     fresh_kv,
     wv,
     wt,
-    wov,
+    wg,
     wot,
     xg,
     tpack,
@@ -92,12 +93,14 @@
     stat_in,
     ctx,
     ctxt,
-    pbuf,
-    half_in,
-    full_in,
+    cx,
+    mine,
+    give,
     last_in,
     tp,
     trx,
+    text_give,
+    text_last,
     send_sem,
     recv_sem,
     local_sem,
@@ -145,21 +148,21 @@
     xp, xm, ylp, sib = at(dx=1), at(dx=3), at(fy=1), at(fc=1)
 
     for s in range(2):
-        def rows(dz, fy, s=s):
-            return xg.at[s, pl.ds(slot_of(dz, fy) * ROWS, ROWS), :]
-
-        def part(dz, fy, cols, s=s):
-            return xg.at[s, pl.ds(slot_of(dz, fy) * ROWS, ROWS), cols]
+        def rows(dz, fy, low=0, high=D, s=s):
+            return xg.at[s, pl.ds(slot_of(dz, fy) * ROWS, ROWS), pl.ds(low, high - low)]
 
         message(("ag", s, 0), rows(0, 0), rows(0, 1), yp)
         message(("ag", s, 1), rows(0, 0), rows(3, 0), zp)
         message(("ag", s, 2), rows(0, 0), rows(1, 0), zm)
-        message(("ag", s, 3), rows(0, 1), rows(3, 1), zp)
-        message(("ag", s, 4), rows(0, 1), rows(1, 1), zm)
-        message(("ag", s, 5), part(3, 0, FIRST), part(2, 0, FIRST), zp)
-        message(("ag", s, 6), part(1, 0, SECOND), part(2, 0, SECOND), zm)
-        message(("ag", s, 7), part(3, 1, FIRST), part(2, 1, FIRST), zp)
-        message(("ag", s, 8), part(1, 1, SECOND), part(2, 1, SECOND), zm)
+        message(("ag", s, 3), rows(0, 1, 0, NEAR), rows(3, 1, 0, NEAR), zp)
+        message(("ag", s, 4), rows(0, 1, 0, NEAR), rows(1, 1, 0, NEAR), zm)
+        message(("ag", s, 5), rows(3, 0, 0, HALF), rows(2, 0, 0, HALF), zp)
+        message(("ag", s, 6), rows(1, 0, HALF, D), rows(2, 0, HALF, D), zm)
+        message(("ag", s, 7), rows(3, 1, 0, NEAR // 2), rows(2, 1, 0, NEAR // 2), zp)
+        message(("ag", s, 8), rows(1, 1, NEAR // 2, NEAR), rows(2, 1, NEAR // 2, NEAR), zm)
+        message(("ag", s, 9), rows(3, 0, NEAR, D), rows(3, 1, NEAR, D), yp)
+        message(("ag", s, 10), rows(1, 0, NEAR, D), rows(1, 1, NEAR, D), yp)
+        message(("ag", s, 11), rows(2, 0, NEAR, D), rows(2, 1, NEAR, D), yp)
 
     def gather_x(kind, block):
         message((kind, 0), block(0, 0), block(0, 1), sib)
@@ -186,32 +189,57 @@
             message(("pc", s, hh), part_out.at[s, hh], part_in.at[s, hh], ylp)
             message(("st", s, hh), stat_out.at[s, hh], stat_in.at[s, hh], ylp)
 
-    others = [(dz, fy) for dz in range(4) for fy in range(2) if (dz, fy) != (0, 0)]
-    for dz, fy in others:
-        message(("ta", dz, fy), tg.at[0], tg.at[slot_of(-dz, fy)], at(fh=fy, dz=dz))
-    for dz, fy in others:
-        message(
-            ("tr", dz, fy), tp.at[slot_of(dz, fy)], trx.at[slot_of(-dz, fy)], at(fh=fy, dz=dz)
-        )
+    message(("ta", 0), tg.at[0], tg.at[slot_of(0, 1)], yp)
+    for dz in range(1, 4):
+        message(("ta", dz), tg.at[0], tg.at[slot_of(-dz, 0)], at(dz=dz))
+        message(("tb", dz), tg.at[slot_of(0, 1)], tg.at[slot_of(-dz, 1)], at(dz=dz))
+        message(("tr", dz), tp.at[pl.ds(slot_of(dz, 0), 2)], trx.at[(-dz) % 4], at(dz=dz))
+    message(("ty",), text_give, text_last, yp)
+
+    def piece_rows(dx, fc):
+        core = 1 - c if fc else c
+        return pl.ds(pl.multiple_of((((x + dx) % 4) * 2 + core) * ROWS, ROWS), ROWS)
+
+    def weights(dx, fc, cols=pl.ds(0, D)):
+        return wg.at[pl.ds(1, 3), piece_rows(dx, fc), cols]
+
+    for part, low in enumerate((0, HALF)):
+        whole, left, right = (low, HALF), (low, HALF // 2), (low + HALF // 2, HALF // 2)
+        for dz in range(1, 4):
+            message(
+                ("wz", part, dz),
+                video_out_w.at[piece_rows(0, 0), pl.ds(*whole)],
+                wg.at[(-dz) % 4, piece_rows(0, 0), pl.ds(*whole)],
+                at(dz=dz),
+            )
+        for i, (where, cols, device) in enumerate(
+            [
+                (0, whole, sib),
+                (0, whole, xp),
+                (0, whole, xm),
+                (3, whole, sib),
+                (3, left, xp),
+                (1, whole, sib),
+                (1, right, xm),
+                (2, whole, sib),
+            ]
+        ):
+            block = weights(where, 0, pl.ds(*cols))
+            message(("wx", part, i), block, block, device)
 
     for s in range(2):
-        for fy in range(2):
-            def summand(dz, s=s, fy=fy):
-                return pbuf.at[s, pl.ds(slot_of(dz, fy) * ROWS, ROWS), :]
-
-            def summand_part(dz, cols, s=s, fy=fy):
-                return pbuf.at[s, pl.ds(slot_of(dz, fy) * ROWS, ROWS), cols]
-
-            message(("rs", s, 0, fy), summand_part(2, FIRST), half_in.at[s, 0, fy], zp)
-            message(("rs", s, 1, fy), summand_part(2, SECOND), half_in.at[s, 1, fy], zm)
-            message(("rs", s, 2, fy), summand(1), full_in.at[s, 0, fy], zp)
-            message(("rs", s, 3, fy), summand(3), full_in.at[s, 1, fy], zm)
-        message(
-            ("rs", s, 4), pbuf.at[s, pl.ds(slot_of(0, 1) * ROWS, ROWS), :], last_in.at[s], yp
-        )
+        for dz in range(1, 4):
+            message(
+                ("cx", s, dz),
+                ctx.at[s, pl.ds(dz * 2 * ROWS, 2 * ROWS), :],
+                cx.at[s, (-dz) % 4],
+                at(dz=dz),
+            )
+        for i, cols in enumerate((FIRST, SECOND)):
+            message(("yo", s, i), give.at[s, :, cols], last_in.at[s, :, cols], yp)
 
     barrier = pltpu.get_barrier_semaphore()
-    peers = [sib, ylp, xp, xm] + [at(fh=fy, dz=dz) for dz, fy in others]
+    peers = [sib, ylp, xp, xm, zp, zm, yp, at(dz=2)]
     for device in peers:
         pl.semaphore_signal(barrier, inc=1, device_id=device, device_id_type=MESH)
 
@@ -228,7 +256,7 @@
     ]
     load_wt = load(text_qkv, wt)
     load_wv = load(video_qkv, wv)
-    load_wov = load(video_out_w, wov)
+    load_wov = load(video_out_w, wg.at[0])
     load_wot = load(text_out_w, wot)
 
     def normalize_video(s):
@@ -248,8 +276,7 @@
     pl.semaphore_wait(barrier, len(peers))
 
     start(("ag", 0, 0), ("ag", 0, 1), ("ag", 0, 2))
-    for dz, fy in others:
-        start(("ta", dz, fy))
+    start(*[("ta", i) for i in range(4)])
     for copy in load_stale:
         copy.wait()
     start(("kv0", 1), ("kv0", 2), ("kv0", 0))
@@ -258,15 +285,29 @@
     def ag_event(s, number):
         waits, sends = [
             ((0,), (3, 4)),
-            ((1, 2), (5, 6)),
+            ((1, 2), (5, 6, 9, 10)),
             ((3, 4), (7, 8)),
-            ((5, 6, 7, 8), ()),
+            ((5, 6), (11,)),
+            ((7, 8, 9, 10, 11), ()),
         ][number]
         arrived(*[("ag", s, i) for i in waits])
         start(*[("ag", s, i) for i in sends])
 
+    def w_event(part, number):
+        if number == 0:
+            arrived(*[("wz", part, dz) for dz in range(1, 4)])
+            start(("wx", part, 1), ("wx", part, 2), ("wx", part, 0))
+        elif number == 1:
+            arrived(("wx", part, 1), ("wx", part, 2))
+            start(("wx", part, 4), ("wx", part, 6), ("wx", part, 3), ("wx", part, 5))
+        elif number == 2:
+            arrived(("wx", part, 4), ("wx", part, 6))
+            start(("wx", part, 7))
+        else:
+            arrived(*[("wx", part, i) for i in (0, 3, 5, 7)])
+
     def project_text():
-        arrived(*[("ta", dz, fy) for dz, fy in others])
+        arrived(*[("ta", dz) for dz in range(1, 4)], *[("tb", dz) for dz in range(1, 4)])
         packed = tg[...].reshape(128, PIECE)
         for piece in range(4):
             tx[:, piece * PIECE : (piece + 1) * PIECE] = jnp.dot(
@@ -351,52 +392,25 @@
             l_here * here + there
         )
         context = context.astype(BF16)
-        ctx[:, hh * HD : (hh + 1) * HD] = context[0:VID]
+        ctx[s, :, hh * HD : (hh + 1) * HD] = context[0:VID]
         ctxt[s * TXT : (s + 1) * TXT, hh * HD : (hh + 1) * HD] = context[VID:QROWS]
 
-    def finish(s):
-        for tile in range(6):
+    def finish(s, part):
+        for tile in range(3 * part, 3 * part + 3):
             cols = slice(tile * 512, (tile + 1) * 512)
-            pbuf[s, :, cols] = jnp.dot(
-                ctx[...], wov[:, cols], preferred_element_type=F32
-            ).astype(BF16)
-
-    def rs_start(s):
-        for fy in (1, 0):
-            start(("rs", s, 0, fy), ("rs", s, 1, fy))
-
-    def rs_pass(s, fy):
-        arrived(("rs", s, 0, fy))
-        near = slice(slot_of(1, fy) * ROWS, (slot_of(1, fy) + 1) * ROWS)
-        pbuf[s, near, 0:HALF] = (
-            pbuf[s, near, 0:HALF].astype(F32) + half_in[s, 0, fy].astype(F32)
-        ).astype(BF16)
-        start(("rs", s, 2, fy))
-        arrived(("rs", s, 1, fy))
-        near = slice(slot_of(3, fy) * ROWS, (slot_of(3, fy) + 1) * ROWS)
-        pbuf[s, near, HALF:D] = (
-            pbuf[s, near, HALF:D].astype(F32) + half_in[s, 1, fy].astype(F32)
-        ).astype(BF16)
-        start(("rs", s, 3, fy))
-
-    def rs_across(s):
-        arrived(("rs", s, 2, 1), ("rs", s, 3, 1))
-        mine = slice(slot_of(0, 1) * ROWS, (slot_of(0, 1) + 1) * ROWS)
-        pbuf[s, mine, :] = (
-            pbuf[s, mine, :].astype(F32)
-            + full_in[s, 0, 1].astype(F32)
-            + full_in[s, 1, 1].astype(F32)
-        ).astype(BF16)
-        start(("rs", s, 4))
-
-    def rs_end(s):
-        arrived(("rs", s, 2, 0), ("rs", s, 3, 0), ("rs", s, 4))
-        summed = (
-            pbuf[s, 0:ROWS, :].astype(F32)
-            + full_in[s, 0, 0].astype(F32)
-            + full_in[s, 1, 0].astype(F32)
-            + last_in[s].astype(F32)
-        )
+            total = jnp.dot(ctx[s, 0 : 2 * ROWS, :], wg[0, :, cols], preferred_element_type=F32)
+            for dz in range(1, 4):
+                total = total + jnp.dot(cx[s, dz], wg[dz, :, cols], preferred_element_type=F32)
+            mine[s, :, cols] = total[0:ROWS]
+            give[s, :, cols] = total[ROWS : 2 * ROWS].astype(BF16)
+        start(("yo", s, part))
+
+    def contexts_arrived(s):
+        arrived(*[("cx", s, dz) for dz in range(1, 4)])
+
+    def video_end(s):
+        arrived(("yo", s, 0), ("yo", s, 1))
+        summed = mine[s] + last_in[s].astype(F32)
         video_out[s] = (video_in[s].astype(F32) + video_mod[2, s : s + 1, :] * summed).astype(BF16)
 
     def text_sums():
@@ -412,15 +426,20 @@
                 piece_select(piece, True), term, preferred_element_type=F32
             )
         tp[...] = packed.astype(BF16).reshape(8, 16, PIECE)
-        for dz, fy in others:
-            start(("tr", dz, fy))
+        start(*[("tr", dz) for dz in range(1, 4)])
+
+    def text_pass():
+        arrived(*[("tr", dz) for dz in range(1, 4)])
+        summed = tp[0:2].astype(F32)
+        for dz in range(1, 4):
+            summed = summed + trx[dz].astype(F32)
+        tpack[...] = summed[0]
+        text_give[...] = summed[1].astype(BF16)
+        start(("ty",))
 
     def text_end():
-        arrived(*[("tr", dz, fy) for dz, fy in others])
-        summed = tp[0].astype(F32)
-        for dz, fy in others:
-            summed = summed + trx[slot_of(dz, fy)].astype(F32)
-        tpack[...] = summed
+        arrived(("ty",))
+        tpack[...] = tpack[...] + text_last[...].astype(F32)
         for s in range(2):
             rows = jnp.concatenate(
                 [tpack[4 * i + 2 * s : 4 * i + 2 * s + 2, :] for i in range(4)], axis=1
@@ -448,78 +467,90 @@
     ag_event(0, 0)
     start(("ag", 1, 0))
     ag_event(0, 1)
+    start(*[("wz", 0, dz) for dz in range(1, 4)])
+    arrived(("ta", 0))
+    start(("tb", 1), ("tb", 2), ("tb", 3))
+    x_event("kv0", 0)
+    ag_event(0, 2)
+    ag_event(0, 3)
+    w_event(0, 0)
+    x_event("kv0", 1)
+    start(("ag", 1, 1), ("ag", 1, 2))
     project_text()
     start(("tkv", 1), ("tkv", 2), ("tkv", 0))
-    x_event("kv0", 0)
-    ag_event(0, 2)
-    start(("ag", 1, 1), ("ag", 1, 2))
-    x_event("tkv", 0)
-    ag_event(1, 0)
-    x_event("kv0", 1)
-    x_event("tkv", 1)
     load_wv.wait()
-    ag_event(0, 3)
+    ag_event(0, 4)
     project_video(0, 0)
     start(("q", 0, 0), ("q", 0, 1))
     project_video(0, 1)
     project_video(0, 2)
     start(("kv1", 1), ("kv1", 2), ("kv1", 0))
+    ag_event(1, 0)
+    x_event("tkv", 0)
+    arrived(("kv0", 0), ("kv0", 5))
+    attend(0, 0, 0, [own_block(0), groups(0, 1, 4)], True)
+    ag_event(1, 1)
+    start(*[("wz", 1, dz) for dz in range(1, 4)])
+    attend(0, 0, 1, [own_block(0), groups(0, 1, 4)], True)
+    x_event("tkv", 1)
+    ag_event(1, 2)
+    ag_event(1, 3)
+    arrived(("kv0", 3), ("kv0", 7))
+    arrived(("q", 0, 0))
+    attend(0, 1, 0, [groups(0, 0, 4)], True)
+    w_event(0, 1)
     arrived(*[("tkv", i) for i in (0, 3, 5, 7)])
+    attend(0, 1, 0, [groups(0, 4, 8), text_block(0)])
+    give_back(0, 0)
+    arrived(("q", 0, 1))
+    attend(0, 1, 1, [groups(0, 0, 4)], True)
+    x_event("kv1", 0)
+    attend(0, 1, 1, [groups(0, 4, 8), text_block(0)])
+    give_back(0, 1)
     for hh in range(2):
-        attend(0, 0, hh, [own_block(0), text_block(0)], True)
-    arrived(("kv0", 0), ("kv0", 5))
-    ag_event(1, 1)
-    for hh in range(2):
-        attend(0, 0, hh, [groups(0, 1, 4)])
-    arrived(("kv0", 3), ("kv0", 7))
-    for hh in range(2):
-        arrived(("q", 0, hh))
-        attend(0, 1, hh, [groups(0, 0, 4)], True)
-        attend(0, 1, hh, [groups(0, 4, 8), text_block(0)])
-        give_back(0, hh)
-    ag_event(1, 2)
-    x_event("kv1", 0)
-    for hh in range(2):
-        attend(0, 0, hh, [groups(0, 4, 8)])
-    load_wov.wait()
-    for hh in range(2):
-        merge(0, hh)
-    finish(0)
-    rs_start(0)
-    x_event("kv1", 1)
-    ag_event(1, 3)
+        attend(0, 0, hh, [groups(0, 4, 8), text_block(0)])
+    w_event(0, 2)
+    ag_event(1, 4)
     project_video(1, 0)
     start(("q", 1, 0), ("q", 1, 1))
     project_video(1, 1)
     project_video(1, 2)
     fresh_copies = store_fresh()
-    rs_pass(0, 1)
-    rs_pass(0, 0)
+    w_event(1, 0)
+    x_event("kv1", 1)
     for hh in range(2):
-        attend(1, 0, hh, [own_block(1), text_block(1)], True)
+        merge(0, hh)
+    start(*[("cx", 0, dz) for dz in range(1, 4)])
     arrived(("kv1", 0), ("kv1", 5))
     for hh in range(2):
-        attend(1, 0, hh, [groups(1, 1, 4)])
+        attend(1, 0, hh, [own_block(1), groups(1, 1, 4)], True)
     arrived(("kv1", 3), ("kv1", 7))
-    rs_across(0)
     for hh in range(2):
         arrived(("q", 1, hh))
         attend(1, 1, hh, [groups(1, 0, 4)], True)
         attend(1, 1, hh, [groups(1, 4, 8), text_block(1)])
         give_back(1, hh)
+    w_event(1, 1)
     for hh in range(2):
-        attend(1, 0, hh, [groups(1, 4, 8)])
+        attend(1, 0, hh, [groups(1, 4, 8), text_block(1)])
+    load_wov.wait()
+    w_event(0, 3)
+    contexts_arrived(0)
+    finish(0, 0)
     for hh in range(2):
         merge(1, hh)
-    finish(1)
-    rs_start(1)
+    start(*[("cx", 1, dz) for dz in range(1, 4)])
     text_sums()
-    rs_end(0)
-    rs_pass(1, 1)
-    rs_pass(1, 0)
-    rs_across(1)
+    w_event(1, 2)
+    contexts_arrived(1)
+    finish(1, 0)
+    w_event(1, 3)
+    finish(1, 1)
+    finish(0, 1)
+    text_pass()
+    video_end(0)
     text_end()
-    rs_end(1)
+    video_end(1)
     for copy in fresh_copies:
         copy.wait()
     for make in table.values():
@@ -527,15 +558,8 @@
 
 
 def hand_over(*refs):
-    sources, targets, sem = refs[:3], refs[3:6], refs[6]
-    copies = [
-        pltpu.make_async_copy(source, target, sem.at[i])
-        for i, (source, target) in enumerate(zip(sources, targets))
-    ]
-    for copy in copies:
-        copy.start()
-    for copy in copies:
-        copy.wait()
+    for source, target in zip(refs[:3], refs[3:]):
+        target[...] = source[...]
 
 
 def shards(*arrays):
@@ -544,7 +568,7 @@
     scratch = [
         pltpu.VMEM((3, D, 256), BF16),
         pltpu.VMEM((3, D, 256), BF16),
-        pltpu.VMEM((256, D), BF16),
+        pltpu.VMEM((4, 256, D), BF16),
         pltpu.VMEM((256, D), BF16),
         pltpu.VMEM((2, VID, D), BF16),
         pltpu.VMEM((16, PIECE), F32),
@@ -564,16 +588,18 @@
         pltpu.VMEM((2, 2, QROWS, HD), BF16),
         pltpu.VMEM((2, 2, 8, 384), F32),
         pltpu.VMEM((2, 2, 8, 384), F32),
-        pltpu.VMEM((VID, 256), BF16),
+        pltpu.VMEM((2, VID, 256), BF16),
         pltpu.VMEM((2 * TXT, 256), BF16),
-        pltpu.VMEM((2, VID, D), BF16),
-        pltpu.VMEM((2, 2, 2, ROWS, HALF), BF16),
-        pltpu.VMEM((2, 2, 2, ROWS, D), BF16),
+        pltpu.VMEM((2, 4, 2 * ROWS, 256), BF16),
+        pltpu.VMEM((2, ROWS, D), F32),
+        pltpu.VMEM((2, ROWS, D), BF16),
         pltpu.VMEM((2, ROWS, D), BF16),
         pltpu.VMEM((8, 16, PIECE), BF16),
-        pltpu.VMEM((8, 16, PIECE), BF16),
-        pltpu.SemaphoreType.DMA((86,)),
-        pltpu.SemaphoreType.DMA((86,)),
+        pltpu.VMEM((4, 2, 16, PIECE), BF16),
+        pltpu.VMEM((16, PIECE), BF16),
+        pltpu.VMEM((16, PIECE), BF16),
+        pltpu.SemaphoreType.DMA((103,)),
+        pltpu.SemaphoreType.DMA((103,)),
         pltpu.SemaphoreType.DMA((6,)),
         pltpu.SemaphoreType.DMA((16,)),
     ]
@@ -601,9 +627,8 @@
     return pl.pallas_call(
         hand_over,
         out_shape=out_shape,
-        in_specs=[hbm] * 3,
-        out_specs=(hbm,) * 3,
-        scratch_shapes=[pltpu.SemaphoreType.DMA((3,))],
+        in_specs=[vmem] * 3,
+        out_specs=(vmem,) * 3,
     )(*finished)
 
 

time: 101 us -> 78.1 us (0.77)
  Pallas kernels: 100 us -> 77.1 us
    pallas_call x1, Pallas kernels: 21.7 us -> 1.95 us  [shards(): pl.pallas_call(hand_over, out_shape=out_shape, in_specs=[vmem] * 3, out_s...]
    pallas_call x1, Pallas kernels: 78.3 us -> 75.1 us  [shards(): pl.pallas_call(kernel, out_shape=out_shape, in_specs=[vmem, vmem, vmem, v...]
where the time goes in v3:
time: 78.1 us; the launch traced here: 77.7 us
  Pallas kernels  77.1 us (99%)
    pallas_call x1, Pallas kernels, shards(): pl.pallas_call(kernel, out_shape=out_shape, in_specs=[vmem, vmem, vmem, v...  75.1 us
    pallas_call x1, Pallas kernels, shards(): pl.pallas_call(hand_over, out_shape=out_shape, in_specs=[vmem] * 3, out_s...  1.95 us

profile of v3, /device:TPU:0, one launch (start us, length us, event | category | flops | bytes accessed | tf_op | source)
XLA Modules:
  0.0 77.7 jit_solution(11736185378832935818)
XLA Ops:
  0.6 75.1 %shard_map.121 = (bf16[2,32,3072]{2,1,0:T(8,128)(2,1)}, bf16[2,2,3072]{2,1,0:T(2,128)(2,1)}, bf16[2,256,256]{2,1,0:T(8,128)(2,1)}) custom-call(bf16[2,32,3072]{2,1,0:T(8,128)(2,1)} %video_in.1, bf16[2,2,3072]{2,1,0:T(2,128)(2,1)} %text_in.1, f32[3,2,3072]{2,1,0:T(2,128)} %bitcast.2, f32[3,2,3072]{2,1,0:T(2,128)} %bitcast.3, bf16[3,3072,256]{2,1,0:T(8,128)(2,1)} %video_qkv.1, ...), custom_call_target="tpu_custom_call" | custom-call | flops 6000000000 | bytes 16000000 | tf_op jit(solution)/shard_map/pallas_call | solution.py:614
  75.8 1.9 %shard_map.122 = (bf16[2,32,3072]{2,1,0:T(8,128)(2,1)}, bf16[2,2,3072]{2,1,0:T(2,128)(2,1)}, bf16[2,256,256]{2,1,0:T(8,128)(2,1)}) custom-call(bf16[2,32,3072]{2,1,0:T(8,128)(2,1)} %get-tuple-element.6.refs_0_, bf16[2,2,3072]{2,1,0:T(2,128)(2,1)} %get-tuple-element.7.refs_1_, bf16[2,256,256]{2,1,0:T(8,128)(2,1)} %get-tuple-element.8.refs_2_), custom_call_target="tpu_custom_call" | custom-call | tf_op jit(solution)/shard_map/pallas_call | solution.py:627

commit v4 on v3

--- a/solution.py
+++ b/solution.py
@@ -22,7 +22,7 @@
 QROWS = VID + TXT
 PIECE = 768
 
-NEAR = 2048
+NEAR = 1024
 FIRST, SECOND = pl.ds(0, HALF), pl.ds(HALF, HALF)
 
 

time: 78.1 us -> 76 us (0.973)
  Pallas kernels: 77.1 us -> 74.4 us
    pallas_call x1, Pallas kernels: 75.1 us -> 72.4 us  [shards(): pl.pallas_call(kernel, out_shape=out_shape, in_specs=[vmem, vmem, vmem, v...]
where the time goes in v4:
time: 76 us; the launch traced here: 75 us
  Pallas kernels  74.4 us (98%)
    pallas_call x1, Pallas kernels, shards(): pl.pallas_call(kernel, out_shape=out_shape, in_specs=[vmem, vmem, vmem, v...  72.4 us
    pallas_call x1, Pallas kernels, shards(): pl.pallas_call(hand_over, out_shape=out_shape, in_specs=[vmem] * 3, out_s...  1.95 us

profile of v4, /device:TPU:0, one launch (start us, length us, event | category | flops | bytes accessed | tf_op | source)
XLA Modules:
  0.0 75.0 jit_solution(2278524012402157453)
XLA Ops:
  0.6 72.4 %shard_map.121 = (bf16[2,32,3072]{2,1,0:T(8,128)(2,1)}, bf16[2,2,3072]{2,1,0:T(2,128)(2,1)}, bf16[2,256,256]{2,1,0:T(8,128)(2,1)}) custom-call(bf16[2,32,3072]{2,1,0:T(8,128)(2,1)} %video_in.1, bf16[2,2,3072]{2,1,0:T(2,128)(2,1)} %text_in.1, f32[3,2,3072]{2,1,0:T(2,128)} %bitcast.2, f32[3,2,3072]{2,1,0:T(2,128)} %bitcast.3, bf16[3,3072,256]{2,1,0:T(8,128)(2,1)} %video_qkv.1, ...), custom_call_target="tpu_custom_call" | custom-call | flops 6000000000 | bytes 16000000 | tf_op jit(solution)/shard_map/pallas_call | solution.py:614
  73.1 1.9 %shard_map.122 = (bf16[2,32,3072]{2,1,0:T(8,128)(2,1)}, bf16[2,2,3072]{2,1,0:T(2,128)(2,1)}, bf16[2,256,256]{2,1,0:T(8,128)(2,1)}) custom-call(bf16[2,32,3072]{2,1,0:T(8,128)(2,1)} %get-tuple-element.6.refs_0_, bf16[2,2,3072]{2,1,0:T(2,128)(2,1)} %get-tuple-element.7.refs_1_, bf16[2,256,256]{2,1,0:T(8,128)(2,1)} %get-tuple-element.8.refs_2_), custom_call_target="tpu_custom_call" | custom-call | tf_op jit(solution)/shard_map/pallas_call | solution.py:627
